TPU v7x, 32 devices: a whole 2x2x4 slice. The times are simulated.
32 devices in a mesh: vrow: 2 (over y), vcol: 2 (over x), pix: 8 (over z, core).
Axes of the slice: x: 2, y: 2, z: 4, core: 2. Of those that a mesh axis runs over, the one named last changes fastest.
Arguments:
- features: bfloat16 [16, 16, 64, 1024], P('vrow', 'vcol', None, 'pix'), may hold values from -400 to 400
- out_cotangent: bfloat16 [16, 16, 64, 1024], P('vrow', 'vcol', None, 'pix'), may hold values from -6 to 6
- norm_gain: float32 [64], replicated, may hold values from 0.25 to 1.75
- query_proj: bfloat16 [64, 64], replicated, may hold values from -0.75 to 0.75
- keyval_proj: bfloat16 [64, 128], replicated, may hold values from -0.75 to 0.75
- output_proj: bfloat16 [64, 64], replicated, may hold values from -0.75 to 0.75
Outputs:
- features_grad: bfloat16 [16, 16, 64, 1024], P('vrow', 'vcol', None, 'pix')
- query_proj_grad: float32 [64, 64], replicated
- keyval_proj_grad: float32 [64, 128], replicated
- output_proj_grad: float32 [64, 64], replicated
- norm_gain_grad: float32 [64], replicated
All inputs are finite; a program needn't handle non-finite values.
Results may differ from a plain program's by a relative error of at most 0.0085.
Values may be sent and summed in bfloat16 or wider, within the bound.
A program may use at most 128 MiB of HBM per device.

v0:
```python
import math

import jax
import jax.numpy as jnp
from jax import lax
from jax.sharding import PartitionSpec as P

HEADS = 4


EPSILON = 1e-06
precise = lax.Precision.HIGHEST


def extended(shard, sides, width):
    for axis, dim in sides:
        count, length = (lax.axis_size(axis), shard.shape[dim])
        up = [(i, (i + 1) % count) for i in range(count - 1)]
        down = [(j, i) for i, j in up]
        last = lax.slice_in_dim(shard, length - width, length, axis=dim)
        leading = lax.slice_in_dim(shard, 0, width, axis=dim)
        before = lax.ppermute(last, axis, up)
        after = lax.ppermute(leading, axis, down)
        shard = jnp.concatenate([before, shard, after], axis=dim)
    return shard


def normalize(features, norm_gain):
    values = features.astype(jnp.float32)
    inv_norm = lax.rsqrt(jnp.mean(values * values, axis=2, keepdims=True) + EPSILON)
    scaled = values * inv_norm
    normed = (scaled * norm_gain[None, None, :, None]).astype(jnp.bfloat16)
    return (normed, scaled, inv_norm)


def unit_rows(raw_proj):
    inv_norm = lax.rsqrt(jnp.mean(raw_proj * raw_proj, axis=2, keepdims=True) + EPSILON)
    return (raw_proj * inv_norm, inv_norm)


def unit_back(unit_vals, inv_norm, upstream):
    return inv_norm * (upstream - unit_vals * jnp.mean(upstream * unit_vals, axis=2, keepdims=True))


def project(normed, weight):
    return jnp.einsum("uvdp,de->uvep", normed, weight, preferred_element_type=jnp.float32)


def split_heads(grid_data):
    view_rows, view_cols, channels, pixels = grid_data.shape
    return grid_data.astype(jnp.float32).reshape(
        view_rows, view_cols, HEADS, channels // HEADS, pixels
    )


def interior(grid_data):
    return grid_data[2:-2, 2:-2]


def window_at(grid_data, first_row, first_col, view_rows, view_cols):
    zero = jnp.zeros((), jnp.int32)
    starts = (first_row.astype(jnp.int32), first_col.astype(jnp.int32), zero, zero)
    sizes = (view_rows, view_cols, grid_data.shape[2], grid_data.shape[3])
    return lax.dynamic_slice(grid_data, starts, sizes)


def make_tokens(normed, query_proj, keyval_proj):
    channels = normed.shape[2]
    unit_query, query_inv = unit_rows(project(normed, query_proj))
    raw_keyval = project(normed, keyval_proj)
    unit_key, key_inv = unit_rows(raw_keyval[:, :, :channels])
    tokens = jnp.concatenate([unit_query, unit_key, raw_keyval[:, :, channels:]], axis=2).astype(
        jnp.bfloat16
    )
    return (tokens, (unit_query, query_inv, unit_key, key_inv))


def front_halo(normed, query_proj, keyval_proj):
    normed_pad = extended(normed, (("vrow", 0), ("vcol", 1)), 2)
    tokens_pad, stats_pad = make_tokens(normed_pad, query_proj, keyval_proj)
    return (tokens_pad, tuple((interior(statistic) for statistic in stats_pad)))


def side_halo(side_data):
    return extended(side_data, (("vrow", 0), ("vcol", 1)), 2)


def attend(tokens_pad):
    channels = tokens_pad.shape[2] // 3
    own_tokens = interior(tokens_pad)
    view_rows, view_cols = (own_tokens.shape[0], own_tokens.shape[1])
    query_heads = split_heads(own_tokens[:, :, :channels])
    score_scale = (channels // HEADS) ** (-0.5)

    def attend_one_offset(offset, carry):
        exp_total, weighted = carry
        window = window_at(tokens_pad, offset // 5, offset % 5, view_rows, view_cols)
        key_heads = split_heads(window[:, :, channels : 2 * channels])
        values = split_heads(window[:, :, 2 * channels :])
        weight = jnp.exp(jnp.sum(query_heads * key_heads, axis=3) * score_scale)
        return (exp_total + weight, weighted + weight[:, :, :, None] * values)

    initial = (
        jnp.zeros(query_heads.shape[:3] + query_heads.shape[4:], jnp.float32),
        jnp.zeros(query_heads.shape, jnp.float32),
    )
    exp_total, weighted = lax.fori_loop(0, 25, attend_one_offset, initial)
    inv_total = 1.0 / exp_total
    return (query_heads, weighted * inv_total[:, :, :, None], inv_total)


def query_grads(tokens_pad, query_heads, out_heads, inv_total, spread):
    channels = tokens_pad.shape[2] // 3
    view_rows, view_cols, head_count, head_size, pixels = query_heads.shape
    score_scale = head_size ** (-0.5)

    def query_one_offset(offset, query_accum):
        window = window_at(tokens_pad, offset // 5, offset % 5, view_rows, view_cols)
        key_heads = split_heads(window[:, :, channels : 2 * channels])
        values = split_heads(window[:, :, 2 * channels :])
        attn_prob = jnp.exp(jnp.sum(query_heads * key_heads, axis=3) * score_scale) * inv_total
        prob_grad = jnp.sum(out_heads * values, axis=3)
        score_grad = attn_prob * (prob_grad - spread)
        return query_accum + score_grad[:, :, :, None] * key_heads

    query_accum = lax.fori_loop(0, 25, query_one_offset, jnp.zeros(query_heads.shape, jnp.float32))
    return (query_accum * score_scale).reshape(view_rows, view_cols, channels, pixels)


def key_grads(tokens_pad, side_pad):
    channels = tokens_pad.shape[2] // 3
    own_tokens = interior(tokens_pad)
    view_rows, view_cols, pixels = (own_tokens.shape[0], own_tokens.shape[1], own_tokens.shape[3])
    key_heads = split_heads(own_tokens[:, :, channels : 2 * channels])
    values = split_heads(own_tokens[:, :, 2 * channels :])
    score_scale = (channels // HEADS) ** (-0.5)

    def key_one_offset(offset, carry):
        key_accum, value_accum = carry
        first_row = 4 - offset // 5
        first_col = 4 - offset % 5
        queries = split_heads(
            window_at(tokens_pad, first_row, first_col, view_rows, view_cols)[:, :, :channels]
        )
        side_data = window_at(side_pad, first_row, first_col, view_rows, view_cols)
        out_heads = side_data[:, :, :channels].reshape(key_heads.shape)
        inv_total = side_data[:, :, channels : channels + HEADS]
        spread = side_data[:, :, channels + HEADS :]
        attn_prob = jnp.exp(jnp.sum(queries * key_heads, axis=3) * score_scale) * inv_total
        prob_grad = jnp.sum(out_heads * values, axis=3)
        score_grad = attn_prob * (prob_grad - spread)
        return (
            key_accum + score_grad[:, :, :, None] * queries,
            value_accum + attn_prob[:, :, :, None] * out_heads,
        )

    initial = (jnp.zeros(key_heads.shape, jnp.float32), jnp.zeros(key_heads.shape, jnp.float32))
    key_accum, value_accum = lax.fori_loop(0, 25, key_one_offset, initial)
    key_part = (key_accum * score_scale).reshape(view_rows, view_cols, channels, pixels)
    value_part = value_accum.reshape(view_rows, view_cols, channels, pixels)
    return jnp.concatenate([key_part, value_part], axis=2)


def middle(tokens_pad, cotangent, output_proj, surround):
    query_heads, attended, inv_total = attend(tokens_pad)
    view_rows, view_cols, head_count, head_size, pixels = attended.shape
    channels = head_count * head_size
    mixed_out = attended.reshape(view_rows, view_cols, channels, pixels).astype(jnp.bfloat16)
    out_grad = jnp.einsum(
        "uvep,de->uvdp", cotangent, output_proj, preferred_element_type=jnp.float32
    )
    out_heads = out_grad.reshape(attended.shape)
    spread = jnp.sum(out_heads * attended, axis=3)
    query_grad = query_grads(tokens_pad, query_heads, out_heads, inv_total, spread)
    side_pad = surround(jnp.concatenate([out_grad, inv_total, spread], axis=2))
    keyval_grad = key_grads(tokens_pad, side_pad)
    output_part = jnp.einsum(
        "uvdp,uvep->de", mixed_out, cotangent, preferred_element_type=jnp.float32
    )
    return (query_grad, keyval_grad, output_part)


def backward(normed, norm_stats, query_grad, keyval_grad, query_proj, keyval_proj):
    unit_query, query_inv, unit_key, key_inv = norm_stats
    channels = normed.shape[2]
    raw_query_grad = unit_back(unit_query, query_inv, query_grad)
    raw_keyval_grad = jnp.concatenate(
        [unit_back(unit_key, key_inv, keyval_grad[:, :, :channels]), keyval_grad[:, :, channels:]],
        axis=2,
    )
    normed_grad = jnp.einsum(
        "uvep,de->uvdp", raw_query_grad, query_proj.astype(jnp.float32), precision=precise
    )
    normed_grad = normed_grad + jnp.einsum(
        "uvep,de->uvdp", raw_keyval_grad, keyval_proj.astype(jnp.float32), precision=precise
    )
    normed_float = normed.astype(jnp.float32)
    query_part = jnp.einsum("uvdp,uvep->de", normed_float, raw_query_grad, precision=precise)
    keyval_part = jnp.einsum("uvdp,uvep->de", normed_float, raw_keyval_grad, precision=precise)
    return (normed_grad, query_part, keyval_part)


def norm_back(cotangent, scaled, inv_norm, norm_gain, normed_grad):
    scaled_grad = normed_grad * norm_gain[None, None, :, None]
    gain_part = jnp.sum(normed_grad * scaled, axis=(0, 1, 3))
    branch = inv_norm * (
        scaled_grad - scaled * jnp.mean(scaled_grad * scaled, axis=2, keepdims=True)
    )
    return ((cotangent.astype(jnp.float32) + branch).astype(jnp.bfloat16), gain_part)


def body(features, out_cotangent, norm_gain, query_proj, keyval_proj, output_proj):
    view_rows, view_cols, channels, pixels = features.shape
    block_size = min(pixels, 128)

    def one_block(block_index, loop_state):
        input_grads, weight_sums = loop_state
        normed, scaled, inv_norm = normalize(features, norm_gain)
        tokens_pad, norm_stats = front_halo(normed, query_proj, keyval_proj)
        query_grad, keyval_grad, output_part = middle(
            tokens_pad, out_cotangent, output_proj, side_halo
        )
        normed_grad, query_part, keyval_part = backward(
            normed, norm_stats, query_grad, keyval_grad, query_proj, keyval_proj
        )
        grad_block, gain_part = norm_back(out_cotangent, scaled, inv_norm, norm_gain, normed_grad)
        input_grads = grad_block
        parts = (query_part, keyval_part, output_part, gain_part)
        return (input_grads, tuple((summed + addend for summed, addend in zip(weight_sums, parts))))

    initial = (
        jnp.zeros(features.shape, jnp.bfloat16),
        (
            jnp.zeros((channels, channels), jnp.float32),
            jnp.zeros((channels, 2 * channels), jnp.float32),
            jnp.zeros((channels, channels), jnp.float32),
            jnp.zeros((channels,), jnp.float32),
        ),
    )
    features_grad, weight_sums = lax.fori_loop(0, pixels // block_size, one_block, initial)
    query_part, keyval_part, output_part, gain_part = weight_sums
    summed_grads = lax.psum(
        (query_part, keyval_part, output_part, gain_part), ("vrow", "vcol", "pix")
    )
    tokens_all = (
        view_rows
        * view_cols
        * pixels
        * lax.axis_size("vrow")
        * lax.axis_size("vcol")
        * lax.axis_size("pix")
    )
    factor = 1.0 / math.sqrt(tokens_all)
    return (
        features_grad,
        summed_grads[0] * factor,
        summed_grads[1] * factor,
        summed_grads[2] * factor,
        summed_grads[3] * factor,
    )


def solution(mesh):
    placed = (P("vrow", "vcol", None, "pix"), P("vrow", "vcol", None, "pix"), P(), P(), P(), P())
    return jax.shard_map(
        body,
        mesh=mesh,
        in_specs=placed,
        out_specs=(P("vrow", "vcol", None, "pix"), P(), P(), P(), P()),
        check_vma=False,
    )
```

profile of v0, /device:TPU:0, one launch (start us, length us, event | category | flops | bytes accessed | tf_op | source)
XLA Modules:
  0.0 914.6 jit_solution(10770260123416143346)
XLA Ops:
  11.9 4.9 collective-permute-start
  16.8 4.3 collective-permute-done.1
  23.7 4.6 collective-permute-start.2
  28.4 5.9 collective-permute-done.3
  52.1 152.7 %while.72 = (s32[]{:T(128)}, f32[8,8,4,128]{3,2,1,0:T(4,128)S(1)}, f32[8,8,4,16,128]{4,3,2,1,0:T(8,128)}, bf16[12,12,192,128]{3,2,1,0:T(8,128)(2,1)}, f32[8,8,4,...) while((s32[]{:T(128)}, f32[8,8,4,128]{3,2,1,0:T(4,128)S(1)}, ...), condition=%wide.region_5.6_spmd.clone, body=%wide.region_3.5_spmd.clone.sunk | while | flops 3735575 | bytes 13369703 | solution.py:107
  204.9 4.2 multiply_convert_fusion
  209.1 186.6 %while.73 = (s32[]{:T(128)}, f32[8,8,4,16,128]{4,3,2,1,0:T(8,128)}, bf16[12,12,192,128]{3,2,1,0:T(8,128)(2,1)}, f32[8,8,4,16,128]{4,3,2,1,0:T(8,128)S(1)}, f32[8...) while((s32[]{:T(128)}, f32[8,8,4,16,128]{4,3,2,1,0:T(8,128)}, ...), condition=%wide.region_10.11_spmd.clone, body=%wide.region_7.10_spmd.clone.sunk | while | flops 5308439 | bytes 12583298 | solution.py:126
  227.2 3.8 fusion.61
  403.6 4.6 collective-permute-start.4
  412.4 4.9 collective-permute-done.5
  420.2 4.8 collective-permute-start.6
  431.7 7.3 collective-permute-done.7
  443.7 321.1 %while.74 = (s32[]{:T(128)}, f32[8,8,4,16,128]{4,3,2,1,0:T(8,128)}, f32[8,8,4,16,128]{4,3,2,1,0:T(8,128)S(1)}, bf16[12,12,192,128]{3,2,1,0:T(8,128)(2,1)}, f32[8...) while((s32[]{:T(128)}, f32[8,8,4,16,128]{4,3,2,1,0:T(8,128)}, ...), condition=%wide.region_15.16_spmd.clone, body=%wide.region_12.15_spmd.clone.sunk | while | flops 6357017 | bytes 20185520 | solution.py:158
  443.7 4.6 fusion.62
  456.0 4.6 fusion.62
  462.4 3.8 fusion.64
  468.8 4.6 fusion.62
  475.3 3.8 fusion.64
  481.7 4.6 fusion.62
  488.1 3.8 fusion.64
  494.5 4.6 fusion.62
  501.0 3.8 fusion.64
  507.4 4.6 fusion.62
  513.9 3.8 fusion.64
  520.3 4.6 fusion.62
  526.7 3.8 fusion.64
  533.1 4.6 fusion.62
  539.6 3.8 fusion.64
  546.0 4.6 fusion.62
  552.4 3.8 fusion.64
  558.8 4.6 fusion.62
  565.3 3.8 fusion.64
  571.7 4.6 fusion.62
  578.2 3.8 fusion.64
  584.6 4.6 fusion.62
  591.1 3.8 fusion.64
  597.5 4.7 fusion.62
  604.0 3.8 fusion.64
  610.4 4.7 fusion.62
  616.9 3.8 fusion.64
  623.3 4.6 fusion.62
  629.7 3.8 fusion.64
  636.1 4.6 fusion.62
  642.6 3.8 fusion.64
  649.0 4.6 fusion.62
  655.5 3.8 fusion.64
  661.9 4.6 fusion.62
  668.4 3.8 fusion.64
  674.8 4.6 fusion.62
  681.3 3.8 fusion.64
  687.7 4.6 fusion.62
  694.2 3.8 fusion.64
  700.6 4.6 fusion.62
  707.1 3.8 fusion.64
  713.5 4.6 fusion.62
  719.9 3.8 fusion.64
  726.3 4.6 fusion.62
  732.8 3.8 fusion.64
  739.2 4.6 fusion.62
  745.6 3.8 fusion.64
  752.0 4.6 fusion.62
  758.5 3.8 fusion.64
  774.2 4.4 fusion.20
  782.3 121.5 %all-reduce.3.cloned.1.call-done = (f32[64,64]{1,0:T(8,128)}, f32[64,128]{1,0:T(8,128)}, f32[64,64]{1,0:T(8,128)}, f32[64]{0:T(128)}) async-done(((f32[64,64]{1,0:T(8,128)}, f32[64,128]{1,0:T(8,128)}, f32[64,64]{1,0:T(8,128)}, f32[64]{0:T(128)}), (f32[64,64]{1,0:T(8,128)}, f32[64,128]{1,0:T(8,128)}, f32[64,64]{1,0:T(8,128)}, f32[64]{0:T(128)})) %all-reduce.3.cloned.1.call-update) | async-done | bytes 65808 | tf_op jit(solution)/shard_map/psum | solution.py:242
  (319 shorter events, 515.0 us)
Async XLA Ops:
  7.2 28.4 %copy-start = (bf16[64,128]{1,0:T(8,128)(2,1)S(1)}, bf16[64,128]{1,0:T(8,128)(2,1)}, u32[]{:S(2)}) copy-start(bf16[64,128]{1,0:T(8,128)(2,1)} %param.16) | copy-start | bytes 49156
  7.2 896.7 %all-reduce.3.cloned.1.call-start = ((), (), s32[]{:S(2)}) async-start(), calls=%async_computation | async-start | bytes 197632 | tf_op jit(solution)/shard_map/psum | solution.py:242
  8.8 13.6 %copy-start.12 = (f32[8,8,128]{2,1,0:T(8,128)}, f32[8,8,128]{2,1,0:T(8,128)S(1)}, u32[]{:S(2)}) copy-start(f32[8,8,128]{2,1,0:T(8,128)S(1)} %add_rsqrt_fusion.2) | copy-start | bytes 98308
  10.5 32.3 %copy-start.3 = (bf16[8,8,64,128]{3,2,1,0:T(8,128)(2,1)}, bf16[8,8,64,128]{3,2,1,0:T(8,128)(2,1)S(1)}, u32[]{:S(2)}) copy-start(bf16[8,8,64,128]{3,2,1,0:T(8,128)(2,1)S(1)} %fusion.14) | copy-start | bytes 3145732
  10.6 10.6 %collective-permute-start.1 = (bf16[2,8,64,128]{3,2,1,0:T(8,128)(2,1)S(1)}, bf16[2,8,64,128]{3,2,1,0:T(8,128)(2,1)S(1)}, u32[]{:S(2)}, u32[]{:S(2)}) collective-permute-start(bf16[2,8,64,128]{3,2,1,0:T(8,128)(2,1)S(1)} %get-tuple-element.727), channel_id=1, source_target_pairs={{16,0},{17,1},{18,2},{19,3},{20,4},{21,5},{22,6},{23,7},{24,8},{25... | collective-permute-start | bytes 786440 | tf_op jit(solution)/shard_map/while/body/eval_jaxpr/ppermute | solution.py:23
  11.9 10.4 %collective-permute-start = (bf16[2,8,64,128]{3,2,1,0:T(8,128)(2,1)S(1)}, bf16[2,8,64,128]{3,2,1,0:T(8,128)(2,1)S(1)}, u32[]{:S(2)}, u32[]{:S(2)}) collective-permute-start(bf16[2,8,64,128]{3,2,1,0:T(8,128)(2,1)S(1)} %get-tuple-element.726), channel_id=1, source_target_pairs={{0,16},{1,17},{2,18},{3,19},{4,20},{5,21},{6,22},{7,23},{8,24},{9,... | collective-permute-start | bytes 786440 | tf_op jit(solution)/shard_map/while/body/eval_jaxpr/ppermute | solution.py:22
  22.4 11.9 %collective-permute-start.3 = (bf16[12,2,64,128]{3,2,1,0:T(8,128)(2,1)S(1)}, bf16[12,2,64,128]{3,2,1,0:T(8,128)(2,1)S(1)}, u32[]{:S(2)}, u32[]{:S(2)}) collective-permute-start(bf16[12,2,64,128]{3,2,1,0:T(8,128)(2,1)S(1)} %get-tuple-element.725), channel_id=1, source_target_pairs={{8,0},{9,1},{10,2},{11,3},{12,4},{13,5},{14,6},{15,7},{24,16},{25,... | collective-permute-start | bytes 1179656 | tf_op jit(solution)/shard_map/while/body/eval_jaxpr/ppermute | solution.py:23
  23.7 11.8 %collective-permute-start.2 = (bf16[12,2,64,128]{3,2,1,0:T(8,128)(2,1)S(1)}, bf16[12,2,64,128]{3,2,1,0:T(8,128)(2,1)S(1)}, u32[]{:S(2)}, u32[]{:S(2)}) collective-permute-start(bf16[12,2,64,128]{3,2,1,0:T(8,128)(2,1)S(1)} %get-tuple-element.724), channel_id=1, source_target_pairs={{0,8},{1,9},{2,10},{3,11},{4,12},{5,13},{6,14},{7,15},{16,24},{17,... | collective-permute-start | bytes 1179656 | tf_op jit(solution)/shard_map/while/body/eval_jaxpr/ppermute | solution.py:22
  39.7 3.1 copy-start.16
  52.1 152.7 %copy-start.15 = (bf16[64,64]{1,0:T(8,128)(2,1)S(1)}, bf16[64,64]{1,0:T(8,128)(2,1)}, u32[]{:S(2)}) copy-start(bf16[64,64]{1,0:T(8,128)(2,1)} %param.17) | copy-start | bytes 24580
  397.4 2.3 copy-start.10
  399.7 2.3 copy-start.1
  401.4 6.8 copy-start.9
  402.1 7.8 copy-start.7
  402.2 7.7 copy-start.11
  402.2 15.2 %collective-permute-start.5 = (f32[2,8,72,128]{3,2,1,0:T(8,128)S(1)}, f32[2,8,72,128]{3,2,1,0:T(8,128)S(1)}, u32[]{:S(2)}, u32[]{:S(2)}) collective-permute-start(f32[2,8,72,128]{3,2,1,0:T(8,128)S(1)} %get-tuple-element.721), channel_id=1, source_target_pairs={{16,0},{17,1},{18,2},{19,3},{20,4},{21,5},{22,6},{23,7},{24,8},{25... | collective-permute-start | bytes 1769480 | tf_op jit(solution)/shard_map/while/body/eval_jaxpr/ppermute | solution.py:23
  403.6 14.9 %collective-permute-start.4 = (f32[2,8,72,128]{3,2,1,0:T(8,128)S(1)}, f32[2,8,72,128]{3,2,1,0:T(8,128)S(1)}, u32[]{:S(2)}, u32[]{:S(2)}) collective-permute-start(f32[2,8,72,128]{3,2,1,0:T(8,128)S(1)} %get-tuple-element.720), channel_id=1, source_target_pairs={{0,16},{1,17},{2,18},{3,19},{4,20},{5,21},{6,22},{7,23},{8,24},{9,... | collective-permute-start | bytes 1769480 | tf_op jit(solution)/shard_map/while/body/eval_jaxpr/ppermute | solution.py:22
  418.7 20.2 %collective-permute-start.7 = (f32[12,2,72,128]{3,2,1,0:T(8,128)S(1)}, f32[12,2,72,128]{3,2,1,0:T(8,128)S(1)}, u32[]{:S(2)}, u32[]{:S(2)}) collective-permute-start(f32[12,2,72,128]{3,2,1,0:T(8,128)S(1)} %get-tuple-element.719), channel_id=1, source_target_pairs={{8,0},{9,1},{10,2},{11,3},{12,4},{13,5},{14,6},{15,7},{24,16},{25,... | collective-permute-start | bytes 2654216 | tf_op jit(solution)/shard_map/while/body/eval_jaxpr/ppermute | solution.py:23
  420.2 7.0 copy-start.4
  420.2 20.3 %collective-permute-start.6 = (f32[12,2,72,128]{3,2,1,0:T(8,128)S(1)}, f32[12,2,72,128]{3,2,1,0:T(8,128)S(1)}, u32[]{:S(2)}, u32[]{:S(2)}) collective-permute-start(f32[12,2,72,128]{3,2,1,0:T(8,128)S(1)} %get-tuple-element.718), channel_id=1, source_target_pairs={{0,8},{1,9},{2,10},{3,11},{4,12},{5,13},{6,14},{7,15},{16,24},{17,... | collective-permute-start | bytes 2654216 | tf_op jit(solution)/shard_map/while/body/eval_jaxpr/ppermute | solution.py:22
  431.7 12.0 %copy-start.2 = (f32[8,8,4,16,128]{4,3,2,1,0:T(8,128)S(1)}, f32[8,8,4,16,128]{4,3,2,1,0:T(8,128)}, u32[]{:S(2)}) copy-start(f32[8,8,4,16,128]{4,3,2,1,0:T(8,128)} %custom-call.4) | copy-start | bytes 6291460
  766.6 2.2 copy-start.14
  771.0 3.2 copy-start.5
  771.0 3.2 copy-start.8
  771.0 3.2 copy-start.13
  771.0 3.2 copy-start.17
  774.2 4.5 copy-start.6
Sparse Core Ops, SparseCore 0:
  778.8 124.9 all-reduce.2
where the time goes:
time: 919 us; the launch traced here: 915 us
  other arithmetic  655 us (71%)
  waiting for transfers between devices  149 us (16%)
  local copies, waits for them, and re-layouts  49.6 us (5%)
  starting transfers between devices  24.4 us (3%)
  matrix products  19.6 us (2%)
  between operations  14.5 us (2%)
    psum x1, waiting for transfers between devices, body(): lax.psum((query_part, keyval_part, output_part, gain_part), ('vrow', 'vco...  122 us
    reduce_sum x25, other arithmetic, key_one_offset(): jnp.sum(queries * key_heads, axis=3) * score_scale  116 us
    add x25, other arithmetic, key_one_offset(): key_accum + score_grad[:, :, :, None] * queries  94.2 us
    add x25, other arithmetic, query_one_offset(): return query_accum + score_grad[:, :, :, None] * key_heads  93.8 us
    reduce_sum x25, other arithmetic, query_one_offset(): jnp.sum(query_heads * key_heads, axis=3) * score_scale  90.1 us
    add x25, other arithmetic, attend_one_offset(): return (exp_total + weight, weighted + weight[:, :, :, None] * values)  87.3 us
    add x25, other arithmetic, key_one_offset(): value_accum + attn_prob[:, :, :, None] * out_heads  63.5 us
    mul x25, other arithmetic, key_one_offset(): score_grad = attn_prob * (prob_grad - spread)  45.6 us
  transfers between devices with their start and end apart: 9, of which 9 were waited for; matrix products, arithmetic and copies ran while one was open for 2% of the time, Pallas kernels for 0%

commit v1 on v0

v1 whole, which is shorter than its diff:
```python
import functools
import math

import jax
import jax.numpy as jnp
from jax import lax
from jax.experimental import pallas as pl
from jax.experimental.pallas import tpu as pltpu
from jax.sharding import PartitionSpec as P

HEADS = 4
REACH = 2
SPAN = 2 * REACH + 1
EPSILON = 1e-06
f32, bf16 = jnp.float32, jnp.bfloat16


def shift(block, axis, up):
    count = lax.axis_size(axis)
    pairs = [(i, i + 1) if up else (i + 1, i) for i in range(count - 1)]
    return lax.ppermute(block, axis, pairs)


def lanes(ref, row, cols):
    return jnp.concatenate([ref[row, c] for c in cols], axis=1)


def unit_inv(raw):
    return lax.rsqrt(jnp.mean(raw * raw, axis=0, keepdims=True) + EPSILON)


def matmul(a, b):
    return jnp.dot(a, b, preferred_element_type=f32)


def matmul_nt(a, b):
    return lax.dot_general(a, b, (((1,), (1,)), ((), ())), preferred_element_type=f32)


def normalized(x, gain):
    inv = lax.rsqrt(jnp.mean(x * x, axis=0, keepdims=True) + EPSILON)
    scaled = x * inv
    return (scaled * gain).astype(bf16), scaled, inv


def attend_kernel(
    feat, cot, gain, w_t, wo, dq_out, att_out, dkv_out, q_s, g_s, kv_s, dkv_s, w_s, dp_s, dq_s, att_s
):
    rows, cols, chans, pix = cot.shape
    rows_p, cols_p = feat.shape[:2]
    size = chans // HEADS
    scale = size ** (-0.5)
    kv_row = 2 * chans * cols_p
    q_row = chans * cols
    own = range(REACH, REACH + cols)

    def front(row, _):
        x = lanes(feat, row, range(cols_p)).astype(f32)
        normed, _, _ = normalized(x, gain[...])
        raw = matmul(w_t[...], normed)
        raw_q, raw_k, value = raw[:chans], raw[chans : 2 * chans], raw[2 * chans :]
        query = (raw_q * unit_inv(raw_q)).astype(bf16).astype(f32)
        key = (raw_k * unit_inv(raw_k)).astype(bf16).astype(f32)
        value = value.astype(bf16).astype(f32)
        for c in range(cols_p):
            at = slice(c * pix, (c + 1) * pix)
            kv_s[pl.ds(row * kv_row + c, chans, stride=cols_p), :] = key[:, at]
            kv_s[pl.ds(row * kv_row + chans * cols_p + c, chans, stride=cols_p), :] = value[:, at]
        for i, c in enumerate(own):
            q_s[pl.ds(row * q_row + i, chans, stride=cols), :] = query[:, c * pix : (c + 1) * pix]
        dkv_s[pl.ds(row * kv_row, kv_row), :] = jnp.zeros((kv_row, pix), f32)
        return 0

    lax.fori_loop(0, rows_p, front, 0)

    def grads(row, _):
        out_grad = matmul(wo[...], lanes(cot, row, range(cols)))
        for i in range(cols):
            g_s[pl.ds(row * q_row + i, chans, stride=cols), :] = out_grad[:, i * pix : (i + 1) * pix]
        return 0

    lax.fori_loop(0, rows, grads, 0)

    def one(step, _):
        row, head = step // HEADS, step % HEADS
        q_at = (row + REACH) * q_row + head * size * cols
        g_at = row * q_row + head * size * cols
        q = [q_s[pl.ds(q_at + c * cols, cols), :] for c in range(size)]
        g = [g_s[pl.ds(g_at + c * cols, cols), :] for c in range(size)]
        v_off = chans * cols_p

        def fold(parts):
            while len(parts) > 1:
                parts = [a + b for a, b in zip(parts[::2], parts[1::2])]
            return parts[0]

        def forward(a, carry):
            total, w_dp, att = carry
            base = (row + a) * kv_row + head * size * cols_p
            for b in range(SPAN):
                def k(c):
                    return kv_s[pl.ds(base + (b + c * cols_p), cols), :]

                def v(c):
                    return kv_s[pl.ds(base + (v_off + b + c * cols_p), cols), :]

                w = jnp.exp(fold([q[c] * k(c) for c in range(size)]) * scale)
                dp = fold([g[c] * v(c) for c in range(size)])
                att = [att[c] + w * v(c) for c in range(size)]
                total = total + w
                w_dp = w_dp + w * dp
                at = pl.ds((a * SPAN + b) * cols, cols)
                w_s[at, :] = w
                dp_s[at, :] = dp
            return total, w_dp, att

        zero = jnp.zeros((cols, pix), f32)
        total, w_dp, att = lax.fori_loop(0, SPAN, forward, (zero, zero, [zero] * size))
        inv = 1.0 / total
        spread = w_dp * inv
        for c in range(size):
            att_s[pl.ds(g_at + c * cols, cols), :] = att[c] * inv

        def back(a, dq):
            base = (row + a) * kv_row + head * size * cols_p
            for b in range(SPAN):
                at = pl.ds((a * SPAN + b) * cols, cols)
                p = w_s[at, :] * inv
                ds = p * (dp_s[at, :] - spread) * scale
                dq = [dq[c] + ds * kv_s[pl.ds(base + (b + c * cols_p), cols), :] for c in range(size)]
                for c in range(size):
                    dkv_s[pl.ds(base + (b + c * cols_p), cols), :] += ds * q[c]
                for c in range(size):
                    dkv_s[pl.ds(base + (v_off + b + c * cols_p), cols), :] += p * g[c]
            return dq

        dq = lax.fori_loop(0, SPAN, back, [zero] * size)
        for c in range(size):
            dq_s[pl.ds(g_at + c * cols, cols), :] = dq[c]
        return 0

    lax.fori_loop(0, rows * HEADS, one, 0)

    def finish(row, _):
        for i in range(cols):
            dq_out[row, i] = dq_s[pl.ds(row * q_row + i, chans, stride=cols), :].astype(bf16)
            att_out[row, i] = att_s[pl.ds(row * q_row + i, chans, stride=cols), :].astype(bf16)
        return 0

    lax.fori_loop(0, rows, finish, 0)

    def finish_kv(row, _):
        for c in range(cols_p):
            dkv_out[row, c] = dkv_s[pl.ds(row * kv_row + c, 2 * chans, stride=cols_p), :].astype(bf16)
        return 0

    lax.fori_loop(0, rows_p, finish_kv, 0)


def attend(feat_pad, cot, gain, w_t, wo):
    rows, cols, chans, pix = cot.shape
    rows_p, cols_p = feat_pad.shape[:2]
    own = rows * chans * cols
    pad_kv = rows_p * 2 * chans * cols_p
    whole = pl.BlockSpec(memory_space=pltpu.VMEM)
    return pl.pallas_call(
        attend_kernel,
        out_shape=(
            jax.ShapeDtypeStruct(cot.shape, bf16),
            jax.ShapeDtypeStruct(cot.shape, bf16),
            jax.ShapeDtypeStruct((rows_p, cols_p, 2 * chans, pix), bf16),
        ),
        in_specs=[whole] * 5,
        out_specs=(whole,) * 3,
        scratch_shapes=[
            pltpu.VMEM((rows_p * chans * cols, pix), f32),
            pltpu.VMEM((own, pix), f32),
            pltpu.VMEM((pad_kv, pix), f32),
            pltpu.VMEM((pad_kv, pix), f32),
            pltpu.VMEM((SPAN * SPAN * cols, pix), f32),
            pltpu.VMEM((SPAN * SPAN * cols, pix), f32),
            pltpu.VMEM((own, pix), f32),
            pltpu.VMEM((own, pix), f32),
        ],
        compiler_params=pltpu.CompilerParams(vmem_limit_bytes=56 * 2**20),
        name="attend",
    )(feat_pad, cot, gain, w_t, wo)


def back_kernel(factor, feat, cot, dq, dkv, att, gain, w_t, w_all, grad_out, sums_out):
    cols, chans = feat.shape[1], feat.shape[2]
    step = pl.program_id(0)

    @pl.when(step == 0)
    def _():
        sums_out[...] = jnp.zeros_like(sums_out)

    x = lanes(feat, 0, range(cols)).astype(f32)
    normed, scaled, inv = normalized(x, gain[...])
    raw = matmul(w_t[...], normed)

    def unit_back(part, grad):
        part_inv = unit_inv(part)
        unit = part * part_inv
        return part_inv * (grad - unit * jnp.mean(grad * unit, axis=0, keepdims=True))

    d_kv = lanes(dkv, 0, range(cols)).astype(f32)
    d_query = unit_back(raw[:chans], lanes(dq, 0, range(cols)).astype(f32))
    d_key = unit_back(raw[chans : 2 * chans], d_kv[:chans])
    raw_grad = jnp.concatenate([d_query, d_key, d_kv[chans:]], axis=0).astype(bf16)
    normed_grad = matmul(w_all[...], raw_grad)
    m = normed_grad * gain[...]
    cot_block = lanes(cot, 0, range(cols))
    branch = inv * (m - scaled * jnp.mean(m * scaled, axis=0, keepdims=True))
    out = (cot_block.astype(f32) + branch).astype(bf16)
    pix = feat.shape[3]
    for c in range(cols):
        grad_out[0, c] = out[:, c * pix : (c + 1) * pix]
    weight = jnp.concatenate(
        [matmul_nt(normed, raw_grad), matmul_nt(lanes(att, 0, range(cols)), cot_block)], axis=1
    )
    sums_out[:chans, :] += weight * factor
    ones = jnp.ones((8, cols * pix), bf16)
    sums_out[chans:, :chans] += matmul_nt(ones, (normed_grad * scaled).astype(bf16)) * factor


def back(factor, feat, cot, dq, dkv, att, gain, w_t, w_all):
    rows, cols, chans, pix = feat.shape

    def by_row(width):
        return pl.BlockSpec((1, cols, width, pix), lambda r: (r, 0, 0, 0))

    def fixed(array):
        return pl.BlockSpec(array.shape, lambda r: (0, 0))

    sums = jax.ShapeDtypeStruct((chans + 8, 4 * chans), f32)
    return pl.pallas_call(
        functools.partial(back_kernel, factor),
        grid=(rows,),
        out_shape=(jax.ShapeDtypeStruct(feat.shape, bf16), sums),
        in_specs=[by_row(chans), by_row(chans), by_row(chans), by_row(2 * chans), by_row(chans)]
        + [fixed(gain), fixed(w_t), fixed(w_all)],
        out_specs=(by_row(chans), fixed(sums)),
        compiler_params=pltpu.CompilerParams(vmem_limit_bytes=32 * 2**20),
        name="back",
    )(feat, cot, dq, dkv, att, gain, w_t, w_all)


def extended(block, axis, dim):
    length = block.shape[dim]
    before = shift(lax.slice_in_dim(block, length - REACH, length, axis=dim), axis, True)
    after = shift(lax.slice_in_dim(block, 0, REACH, axis=dim), axis, False)
    return jnp.concatenate([before, block, after], axis=dim)


def folded(block, axis, dim):
    length = block.shape[dim]
    to_before = lax.slice_in_dim(block, 0, REACH, axis=dim)
    to_after = lax.slice_in_dim(block, length - REACH, length, axis=dim)
    from_after = shift(to_before, axis, False)
    from_before = shift(to_after, axis, True)
    own = lax.slice_in_dim(block, REACH, length - REACH, axis=dim)
    first = (slice(None),) * dim + (slice(0, REACH),)
    last = (slice(None),) * dim + (slice(own.shape[dim] - REACH, None),)
    return own.at[first].add(from_before).at[last].add(from_after)


def body(features, out_cotangent, norm_gain, query_proj, keyval_proj, output_proj):
    gain = norm_gain[:, None]
    w_all = jnp.concatenate([query_proj, keyval_proj], axis=1)
    w_t = w_all.T
    feat_pad = extended(extended(features, "vrow", 0), "vcol", 1)
    dq, att, dkv = attend(feat_pad, out_cotangent, gain, w_t, output_proj)
    dkv = folded(folded(dkv, "vcol", 1), "vrow", 0)
    rows, cols, chans, pix = features.shape
    axes = ("vrow", "vcol", "pix")
    tokens_all = rows * cols * pix * math.prod(lax.axis_size(a) for a in axes)
    grad, sums = back(
        tokens_all**-0.5, features, out_cotangent, dq, dkv, att, gain, w_t, w_all
    )
    sums = lax.psum(sums, axes)
    return (
        grad,
        sums[:chans, :chans],
        sums[:chans, chans : 3 * chans],
        sums[:chans, 3 * chans :],
        sums[chans, :chans],
    )


def solution(mesh):
    placed = P("vrow", "vcol", None, "pix")
    return jax.shard_map(
        body,
        mesh=mesh,
        in_specs=(placed, placed, P(), P(), P(), P()),
        out_specs=(placed, P(), P(), P(), P()),
        check_vma=False,
    )
```

time: 919 us -> 258 us (0.28)
  other arithmetic: 655 us -> 4.15 us
  Pallas kernels: 0 us -> 50.7 us
  local copies, waits for them, and re-layouts: 49.6 us -> 12.1 us
  matrix products: 19.6 us -> 0 us
    add x100 -> x0, other arithmetic: 339 us -> none  [the longest x25 94.2 us: key_one_offset(): key_accum + score_grad[:, :, :, None] * queries]
    reduce_sum x79 -> x0, other arithmetic: 230 us -> none  [the longest x25 116 us: key_one_offset(): jnp.sum(queries * key_heads, axis=3) * score_scale]
    mul x57 -> x0, other arithmetic: 59.7 us -> none  [the longest x25 45.6 us: key_one_offset(): score_grad = attn_prob * (prob_grad - spread)]
    pallas_call x0 -> x2, Pallas kernels: none -> 50.7 us  [the longest x1 43.9 us: attend(): pl.pallas_call(attend_kernel, out_shape=(jax.ShapeDtypeStruct(cot.shape,...]
    slice x30 -> x8, local copies, waits for them, and re-layouts: 47.4 us -> 9.25 us  [the longest x2 2.54 us: folded(): own = lax.slice_in_dim(block, REACH, length - REACH, axis=dim)]
    dot_general x8 -> x0, matrix products: 19.6 us -> none  [the longest x1 4.42 us: backward(): jnp.einsum('uvep,de->uvdp', raw_keyval_grad, keyval_proj.astype(jnp.float...]
    ppermute x8, waiting for transfers between devices: 27.7 us -> 40.3 us  [shift(): return lax.ppermute(block, axis, pairs)]
where the time goes in v1:
time: 258 us; the launch traced here: 256 us
  waiting for transfers between devices  158 us (61%)
  Pallas kernels  50.7 us (20%)
  starting transfers between devices  16.6 us (6%)
  between operations  14.3 us (6%)
  local copies, waits for them, and re-layouts  12.1 us (5%)
  other arithmetic  4.15 us (2%)
    psum x1, waiting for transfers between devices, body(): sums = lax.psum(sums, axes)  118 us
    pallas_call x1, Pallas kernels, attend(): pl.pallas_call(attend_kernel, out_shape=(jax.ShapeDtypeStruct(cot.shape,...  43.9 us
    ppermute x8, waiting for transfers between devices, shift(): return lax.ppermute(block, axis, pairs)  40.3 us
    ppermute x8, starting transfers between devices, shift(): return lax.ppermute(block, axis, pairs)  16.5 us
    pallas_call x1, Pallas kernels, back(): pl.pallas_call(functools.partial(back_kernel, factor), grid=(rows,), out_...  6.77 us
  transfers between devices with their start and end apart: 9, of which 9 were waited for; matrix products, arithmetic and copies ran while one was open for 2% of the time, Pallas kernels for 0%

profile of v1, /device:TPU:0, one launch (start us, length us, event | category | flops | bytes accessed | tf_op | source)
XLA Modules:
  0.0 256.0 jit_solution(11113628191801813475)
XLA Ops:
  7.2 0.0 copy-start
  7.2 0.0 all-reduce.2.cloned.1.call-start
  7.2 1.1 fusion.7
  8.4 4.9 %collective-permute-start = (bf16[2,8,64,128]{3,2,1,0:T(8,128)(2,1)S(1)}, bf16[2,8,64,128]{3,2,1,0:T(8,128)(2,1)S(1)}, u32[]{:S(2)}, u32[]{:S(2)}) collective-permute-start(bf16[2,8,64,128]{3,2,1,0:T(8,128)(2,1)S(1)} %get-tuple-element.70), channel_id=1, source_target_pairs={{0,16},{1,17},{2,18},{3,19},{4,20},{5,21},{6,22},{7,23},{8,24},{9,... | collective-permute-start | bytes 786440 | tf_op jit(solution)/shard_map/ppermute | solution.py:21
  13.3 1.3 collective-permute-start.1
  14.6 4.2 %collective-permute-done = bf16[2,8,64,128]{3,2,1,0:T(8,128)(2,1)S(1)} collective-permute-done((bf16[2,8,64,128]{3,2,1,0:T(8,128)(2,1)S(1)}, bf16[2,8,64,128]{3,2,1,0:T(8,128)(2,1)S(1)}, u32[]{:S(2)}, u32[]{:S(2)}) %collective-permute-start) | collective-permute-done | bytes 262176 | tf_op jit(solution)/shard_map/ppermute | solution.py:21
  18.8 0.0 copy-done
  18.8 0.0 copy-start.8
  18.8 0.0 copy-start.6
  18.8 0.0 copy-start.7
  18.9 0.1 constant_dynamic-update-slice_fusion.1
  19.0 3.9 %collective-permute-done.1 = bf16[2,8,64,128]{3,2,1,0:T(8,128)(2,1)S(1)} collective-permute-done((bf16[2,8,64,128]{3,2,1,0:T(8,128)(2,1)S(1)}, bf16[2,8,64,128]{3,2,1,0:T(8,128)(2,1)S(1)}, u32[]{:S(2)}, u32[]{:S(2)}) %collective-permute-start.1) | collective-permute-done | bytes 262176 | tf_op jit(solution)/shard_map/ppermute | solution.py:21
  23.0 0.9 fusion.6
  23.9 3.4 %collective-permute-start.2 = (bf16[12,2,64,128]{3,2,1,0:T(8,128)(2,1)}, bf16[12,2,64,128]{3,2,1,0:T(8,128)(2,1)S(1)}, u32[]{:S(2)}, u32[]{:S(2)}) collective-permute-start(bf16[12,2,64,128]{3,2,1,0:T(8,128)(2,1)} %get-tuple-element.67), channel_id=1, source_target_pairs={{0,8},{1,9},{2,10},{3,11},{4,12},{5,13},{6,14},{7,15},{16,24},{17,... | collective-permute-start | bytes 1179656 | tf_op jit(solution)/shard_map/ppermute | solution.py:21
  27.3 1.3 collective-permute-start.3
  28.6 0.0 copy-done.8
  28.6 0.7 copy.11.gain
  29.3 0.0 copy-done.6
  29.3 0.0 copy-done.7
  29.3 0.1 pad_maximum_fusion.1
  29.4 0.7 copy.12.w_t
  30.1 4.6 %collective-permute-done.2 = bf16[12,2,64,128]{3,2,1,0:T(8,128)(2,1)S(1)} collective-permute-done((bf16[12,2,64,128]{3,2,1,0:T(8,128)(2,1)}, bf16[12,2,64,128]{3,2,1,0:T(8,128)(2,1)S(1)}, u32[]{:S(2)}, u32[]{:S(2)}) %collective-permute-start.2) | collective-permute-done | bytes 393248 | tf_op jit(solution)/shard_map/ppermute | solution.py:21
  34.8 4.0 %collective-permute-done.3 = bf16[12,2,64,128]{3,2,1,0:T(8,128)(2,1)S(1)} collective-permute-done((bf16[12,2,64,128]{3,2,1,0:T(8,128)(2,1)}, bf16[12,2,64,128]{3,2,1,0:T(8,128)(2,1)S(1)}, u32[]{:S(2)}, u32[]{:S(2)}) %collective-permute-start.3) | collective-permute-done | bytes 393248 | tf_op jit(solution)/shard_map/ppermute | solution.py:21
  38.8 1.7 pad_maximum_fusion.feat
  40.5 43.9 %attend.1 = (bf16[8,8,64,128]{3,2,1,0:T(8,128)(2,1)}, bf16[8,8,64,128]{3,2,1,0:T(8,128)(2,1)}, bf16[12,12,128,128]{3,2,1,0:T(8,128)(2,1)}) custom-call(bf16[12,12,64,128]{3,2,1,0:T(8,128)(2,1)} %pad_maximum_fusion.feat, bf16[8,8,64,128]{3,2,1,0:T(8,128)(2,1)} %cot.3, f32[64,1]{1,0:T(8,128)} %copy.11.gain, bf16[192,64]{1,0:T(8,128)(2,1)} %copy.12.w_t, ...), custom_call_target="tpu_custom_call" | custom-call | tf_op jit(solution)/shard_map/attend/pallas_call | solution.py:166
  84.4 1.5 fusion.4
  86.0 1.6 collective-permute-start.4
  87.6 1.3 collective-permute-start.5
  88.9 2.3 slice.164
  91.2 10.8 %collective-permute-done.4 = bf16[12,2,128,128]{3,2,1,0:T(8,128)(2,1)S(1)} collective-permute-done((bf16[12,2,128,128]{3,2,1,0:T(8,128)(2,1)S(1)}, bf16[12,2,128,128]{3,2,1,0:T(8,128)(2,1)S(1)}, u32[]{:S(2)}, u32[]{:S(2)}) %collective-permute-start.4) | collective-permute-done | bytes 786464 | tf_op jit(solution)/shard_map/ppermute | solution.py:21
  101.9 1.5 add_dynamic-update-slice_fusion
  103.4 2.7 %collective-permute-done.5 = bf16[12,2,128,128]{3,2,1,0:T(8,128)(2,1)S(1)} collective-permute-done((bf16[12,2,128,128]{3,2,1,0:T(8,128)(2,1)S(1)}, bf16[12,2,128,128]{3,2,1,0:T(8,128)(2,1)S(1)}, u32[]{:S(2)}, u32[]{:S(2)}) %collective-permute-start.5) | collective-permute-done | bytes 786464 | tf_op jit(solution)/shard_map/ppermute | solution.py:21
  106.1 0.4 fusion
  106.5 0.1 fusion.5
  106.6 1.5 collective-permute-start.6
  108.1 1.3 collective-permute-start.7
  109.4 0.0 copy-start.4
  109.4 0.0 copy-start.5
  109.4 0.2 slice.181
  109.7 0.0 copy-start.1
  109.7 0.0 copy-start.2
  109.7 0.0 copy-start.3
  109.7 6.1 %collective-permute-done.6 = bf16[2,8,128,128]{3,2,1,0:T(8,128)(2,1)S(1)} collective-permute-done((bf16[2,8,128,128]{3,2,1,0:T(8,128)(2,1)S(1)}, bf16[2,8,128,128]{3,2,1,0:T(8,128)(2,1)S(1)}, u32[]{:S(2)}, u32[]{:S(2)}) %collective-permute-start.6) | collective-permute-done | bytes 524320 | tf_op jit(solution)/shard_map/ppermute | solution.py:21
  115.8 0.2 fusion.2
  116.0 3.9 %collective-permute-done.7 = bf16[2,8,128,128]{3,2,1,0:T(8,128)(2,1)S(1)} collective-permute-done((bf16[2,8,128,128]{3,2,1,0:T(8,128)(2,1)S(1)}, bf16[2,8,128,128]{3,2,1,0:T(8,128)(2,1)S(1)}, u32[]{:S(2)}, u32[]{:S(2)}) %collective-permute-start.7) | collective-permute-done | bytes 524320 | tf_op jit(solution)/shard_map/ppermute | solution.py:21
  119.9 0.3 fusion.1.dkv
  120.2 0.0 copy-done.4
  120.2 0.0 copy-done.5
  120.2 0.0 copy-done.1
  120.3 0.0 copy-done.2
  120.3 0.0 copy-done.3
  120.3 6.8 %back.1 = (bf16[8,8,64,128]{3,2,1,0:T(8,128)(2,1)}, f32[72,256]{1,0:T(8,128)}) custom-call(bf16[8,8,64,128]{3,2,1,0:T(8,128)(2,1)S(1)} %copy-done, bf16[8,8,64,128]{3,2,1,0:T(8,128)(2,1)S(1)} %copy-done.1, bf16[8,8,64,128]{3,2,1,0:T(8,128)(2,1)S(1)} %copy-done.2, bf16[8,8,128,128]{3,2,1,0:T(8,128)(2,1)S(1)} %fusion.1.dkv, ...), custom_call_target="tpu_custom_call" | custom-call | tf_op jit(solution)/shard_map/back/pallas_call | solution.py:237
  127.1 0.0 all-reduce.2.cloned.1.call-update
  127.1 117.8 %all-reduce.2.cloned.1.call-done = f32[72,256]{1,0:T(8,128)} async-done(((f32[72,256]{1,0:T(8,128)}), f32[72,256]{1,0:T(8,128)}) %all-reduce.2.cloned.1.call-update) | async-done | bytes 73744 | tf_op jit(solution)/shard_map/psum | solution.py:281
  244.9 1.2 slice_bitcast_fusion
  246.1 1.5 slice.187
  247.6 1.5 fusion.8
  (2 shorter events, 0.1 us)
Async XLA Ops:
  7.2 11.7 %copy-start = (bf16[8,8,64,128]{3,2,1,0:T(8,128)(2,1)S(1)}, bf16[8,8,64,128]{3,2,1,0:T(8,128)(2,1)}, u32[]{:S(2)}) copy-start(bf16[8,8,64,128]{3,2,1,0:T(8,128)(2,1)} %feat.1) | copy-start | bytes 3145732
  7.2 237.8 %all-reduce.2.cloned.1.call-start = ((), (), s32[]{:S(2)}) async-start(), calls=%async_computation | async-start | bytes 147456 | tf_op jit(solution)/shard_map/psum | solution.py:281
  8.4 10.4 %collective-permute-start = (bf16[2,8,64,128]{3,2,1,0:T(8,128)(2,1)S(1)}, bf16[2,8,64,128]{3,2,1,0:T(8,128)(2,1)S(1)}, u32[]{:S(2)}, u32[]{:S(2)}) collective-permute-start(bf16[2,8,64,128]{3,2,1,0:T(8,128)(2,1)S(1)} %get-tuple-element.70), channel_id=1, source_target_pairs={{0,16},{1,17},{2,18},{3,19},{4,20},{5,21},{6,22},{7,23},{8,24},{9,... | collective-permute-start | bytes 786440 | tf_op jit(solution)/shard_map/ppermute | solution.py:21
  13.3 9.7 %collective-permute-start.1 = (bf16[2,8,64,128]{3,2,1,0:T(8,128)(2,1)S(1)}, bf16[2,8,64,128]{3,2,1,0:T(8,128)(2,1)S(1)}, u32[]{:S(2)}, u32[]{:S(2)}) collective-permute-start(bf16[2,8,64,128]{3,2,1,0:T(8,128)(2,1)S(1)} %get-tuple-element.69), channel_id=1, source_target_pairs={{16,0},{17,1},{18,2},{19,3},{20,4},{21,5},{22,6},{23,7},{24,8},{25... | collective-permute-start | bytes 786440 | tf_op jit(solution)/shard_map/ppermute | solution.py:21
  18.8 9.8 %copy-start.8 = (f32[64]{0:T(128)S(1)}, f32[64]{0:T(128)}, u32[]{:S(2)}) copy-start(f32[64]{0:T(128)} %param.16) | copy-start | bytes 772
  18.8 10.5 %copy-start.6 = (bf16[64,128]{1,0:T(8,128)(2,1)S(1)}, bf16[64,128]{1,0:T(8,128)(2,1)}, u32[]{:S(2)}) copy-start(bf16[64,128]{1,0:T(8,128)(2,1)} %param.18) | copy-start | bytes 49156
  18.8 10.5 %copy-start.7 = (bf16[64,64]{1,0:T(8,128)(2,1)S(1)}, bf16[64,64]{1,0:T(8,128)(2,1)}, u32[]{:S(2)}) copy-start(bf16[64,64]{1,0:T(8,128)(2,1)} %param.17) | copy-start | bytes 24580
  23.9 10.9 %collective-permute-start.2 = (bf16[12,2,64,128]{3,2,1,0:T(8,128)(2,1)}, bf16[12,2,64,128]{3,2,1,0:T(8,128)(2,1)S(1)}, u32[]{:S(2)}, u32[]{:S(2)}) collective-permute-start(bf16[12,2,64,128]{3,2,1,0:T(8,128)(2,1)} %get-tuple-element.67), channel_id=1, source_target_pairs={{0,8},{1,9},{2,10},{3,11},{4,12},{5,13},{6,14},{7,15},{16,24},{17,... | collective-permute-start | bytes 1179656 | tf_op jit(solution)/shard_map/ppermute | solution.py:21
  27.3 11.5 %collective-permute-start.3 = (bf16[12,2,64,128]{3,2,1,0:T(8,128)(2,1)}, bf16[12,2,64,128]{3,2,1,0:T(8,128)(2,1)S(1)}, u32[]{:S(2)}, u32[]{:S(2)}) collective-permute-start(bf16[12,2,64,128]{3,2,1,0:T(8,128)(2,1)} %get-tuple-element.68), channel_id=1, source_target_pairs={{8,0},{9,1},{10,2},{11,3},{12,4},{13,5},{14,6},{15,7},{24,16},{25,... | collective-permute-start | bytes 1179656 | tf_op jit(solution)/shard_map/ppermute | solution.py:21
  86.0 16.0 %collective-permute-start.4 = (bf16[12,2,128,128]{3,2,1,0:T(8,128)(2,1)S(1)}, bf16[12,2,128,128]{3,2,1,0:T(8,128)(2,1)S(1)}, u32[]{:S(2)}, u32[]{:S(2)}) collective-permute-start(bf16[12,2,128,128]{3,2,1,0:T(8,128)(2,1)S(1)} %get-tuple-element.64), channel_id=1, source_target_pairs={{0,8},{1,9},{2,10},{3,11},{4,12},{5,13},{6,14},{7,15},{16,24},{17,... | collective-permute-start | bytes 2359304 | tf_op jit(solution)/shard_map/ppermute | solution.py:21
  87.6 18.5 %collective-permute-start.5 = (bf16[12,2,128,128]{3,2,1,0:T(8,128)(2,1)S(1)}, bf16[12,2,128,128]{3,2,1,0:T(8,128)(2,1)S(1)}, u32[]{:S(2)}, u32[]{:S(2)}) collective-permute-start(bf16[12,2,128,128]{3,2,1,0:T(8,128)(2,1)S(1)} %get-tuple-element.63), channel_id=1, source_target_pairs={{8,0},{9,1},{10,2},{11,3},{12,4},{13,5},{14,6},{15,7},{24,16},{25,... | collective-permute-start | bytes 2359304 | tf_op jit(solution)/shard_map/ppermute | solution.py:21
  106.6 9.2 %collective-permute-start.6 = (bf16[2,8,128,128]{3,2,1,0:T(8,128)(2,1)S(1)}, bf16[2,8,128,128]{3,2,1,0:T(8,128)(2,1)S(1)}, u32[]{:S(2)}, u32[]{:S(2)}) collective-permute-start(bf16[2,8,128,128]{3,2,1,0:T(8,128)(2,1)S(1)} %get-tuple-element.66), channel_id=1, source_target_pairs={{0,16},{1,17},{2,18},{3,19},{4,20},{5,21},{6,22},{7,23},{8,24},{9,... | collective-permute-start | bytes 1572872 | tf_op jit(solution)/shard_map/ppermute | solution.py:21
  108.1 11.8 %collective-permute-start.7 = (bf16[2,8,128,128]{3,2,1,0:T(8,128)(2,1)S(1)}, bf16[2,8,128,128]{3,2,1,0:T(8,128)(2,1)S(1)}, u32[]{:S(2)}, u32[]{:S(2)}) collective-permute-start(bf16[2,8,128,128]{3,2,1,0:T(8,128)(2,1)S(1)} %get-tuple-element.65), channel_id=1, source_target_pairs={{16,0},{17,1},{18,2},{19,3},{20,4},{21,5},{22,6},{23,7},{24,8},{25... | collective-permute-start | bytes 1572872 | tf_op jit(solution)/shard_map/ppermute | solution.py:21
  109.4 10.8 %copy-start.4 = (bf16[192,64]{1,0:T(8,128)(2,1)S(1)}, bf16[192,64]{1,0:T(8,128)(2,1)}, u32[]{:S(2)}) copy-start(bf16[192,64]{1,0:T(8,128)(2,1)} %copy.12.w_t) | copy-start | bytes 73732
  109.4 10.8 %copy-start.5 = (f32[64,1]{1,0:T(8,128)S(1)}, f32[64,1]{1,0:T(8,128)}, u32[]{:S(2)}) copy-start(f32[64,1]{1,0:T(8,128)} %copy.11.gain) | copy-start | bytes 772
  109.7 10.6 %copy-start.1 = (bf16[8,8,64,128]{3,2,1,0:T(8,128)(2,1)S(1)}, bf16[8,8,64,128]{3,2,1,0:T(8,128)(2,1)}, u32[]{:S(2)}) copy-start(bf16[8,8,64,128]{3,2,1,0:T(8,128)(2,1)} %cot.3) | copy-start | bytes 3145732
  109.7 10.6 %copy-start.2 = (bf16[8,8,64,128]{3,2,1,0:T(8,128)(2,1)S(1)}, bf16[8,8,64,128]{3,2,1,0:T(8,128)(2,1)}, u32[]{:S(2)}) copy-start(bf16[8,8,64,128]{3,2,1,0:T(8,128)(2,1)} %get-tuple-element.58.dq) | copy-start | bytes 3145732
  109.7 10.6 %copy-start.3 = (bf16[8,8,64,128]{3,2,1,0:T(8,128)(2,1)S(1)}, bf16[8,8,64,128]{3,2,1,0:T(8,128)(2,1)}, u32[]{:S(2)}) copy-start(bf16[8,8,64,128]{3,2,1,0:T(8,128)(2,1)} %get-tuple-element.60.att) | copy-start | bytes 3145732
Sparse Core Ops, SparseCore 0:
  127.2 117.6 all-reduce.1

commit v2 on v1

--- a/solution.py
+++ b/solution.py
@@ -246,6 +246,19 @@
     )(feat, cot, dq, dkv, att, gain, w_t, w_all)
 
 
+def summed(block, axes):
+    for axis in axes:
+        count = lax.axis_size(axis)
+        if count & (count - 1):
+            block = lax.psum(block, axis)
+            continue
+        hop = 1
+        while hop < count:
+            block = block + lax.ppermute(block, axis, [(i, i ^ hop) for i in range(count)])
+            hop *= 2
+    return block
+
+
 def extended(block, axis, dim):
     length = block.shape[dim]
     before = shift(lax.slice_in_dim(block, length - REACH, length, axis=dim), axis, True)
@@ -278,7 +291,7 @@
     grad, sums = back(
         tokens_all**-0.5, features, out_cotangent, dq, dkv, att, gain, w_t, w_all
     )
-    sums = lax.psum(sums, axes)
+    sums = summed(sums, axes[::-1])
     return (
         grad,
         sums[:chans, :chans],

time: 258 us -> 143 us (0.55)
  waiting for transfers between devices: 158 us -> 55.9 us
  between operations: 14.3 us -> 0.93 us
  starting transfers between devices: 16.6 us -> 21 us
    psum x1 -> x0, waiting for transfers between devices: 118 us -> none  [body(): sums = lax.psum(sums, axes)]
    ppermute x0 -> x5, waiting for transfers between devices: none -> 15.3 us  [summed(): lax.ppermute(block, axis, [(i, i ^ hop) for i in range(count)])]
    ppermute x0 -> x5, starting transfers between devices: none -> 4.48 us  [summed(): lax.ppermute(block, axis, [(i, i ^ hop) for i in range(count)])]
  transfers between devices with their start and end apart: 9 -> 13, of which waited for: 9 -> 13; matrix products, arithmetic and copies ran while one was open for 2% -> 4% of each run, Pallas kernels for 0% -> 0%
where the time goes in v2:
time: 143 us; the launch traced here: 142 us
  waiting for transfers between devices  55.9 us (39%)
  Pallas kernels  50.7 us (35%)
  starting transfers between devices  21 us (15%)
  local copies, waits for them, and re-layouts  9.58 us (7%)
  other arithmetic  4.17 us (3%)
    pallas_call x1, Pallas kernels, attend(): pl.pallas_call(attend_kernel, out_shape=(jax.ShapeDtypeStruct(cot.shape,...  43.9 us
    ppermute x8, waiting for transfers between devices, shift(): return lax.ppermute(block, axis, pairs)  40.5 us
    ppermute x8, starting transfers between devices, shift(): return lax.ppermute(block, axis, pairs)  16.5 us
    ppermute x5, waiting for transfers between devices, summed(): lax.ppermute(block, axis, [(i, i ^ hop) for i in range(count)])  15.3 us
    pallas_call x1, Pallas kernels, back(): pl.pallas_call(functools.partial(back_kernel, factor), grid=(rows,), out_...  6.78 us
    ppermute x5, starting transfers between devices, summed(): lax.ppermute(block, axis, [(i, i ^ hop) for i in range(count)])  4.48 us
  transfers between devices with their start and end apart: 13, of which 13 were waited for; matrix products, arithmetic and copies ran while one was open for 4% of the time, Pallas kernels for 0%

profile of v2, /device:TPU:0, one launch (start us, length us, event | category | flops | bytes accessed | tf_op | source)
XLA Modules:
  0.0 142.3 jit_solution(7897301033496204037)
XLA Ops:
  0.6 0.0 copy-start
  0.6 1.2 fusion.7
  1.8 4.9 %collective-permute-start = (bf16[2,8,64,128]{3,2,1,0:T(8,128)(2,1)S(1)}, bf16[2,8,64,128]{3,2,1,0:T(8,128)(2,1)S(1)}, u32[]{:S(2)}, u32[]{:S(2)}) collective-permute-start(bf16[2,8,64,128]{3,2,1,0:T(8,128)(2,1)S(1)} %get-tuple-element.70), channel_id=1, source_target_pairs={{0,16},{1,17},{2,18},{3,19},{4,20},{5,21},{6,22},{7,23},{8,24},{9,... | collective-permute-start | bytes 786440 | tf_op jit(solution)/shard_map/ppermute | solution.py:21
  6.7 1.3 collective-permute-start.1
  8.0 4.2 %collective-permute-done = bf16[2,8,64,128]{3,2,1,0:T(8,128)(2,1)S(1)} collective-permute-done((bf16[2,8,64,128]{3,2,1,0:T(8,128)(2,1)S(1)}, bf16[2,8,64,128]{3,2,1,0:T(8,128)(2,1)S(1)}, u32[]{:S(2)}, u32[]{:S(2)}) %collective-permute-start) | collective-permute-done | bytes 262176 | tf_op jit(solution)/shard_map/ppermute | solution.py:21
  12.2 0.0 copy-done
  12.3 0.0 copy-start.8
  12.3 0.0 copy-start.6
  12.3 0.0 copy-start.7
  12.3 0.2 constant_dynamic-update-slice_fusion.1
  12.5 3.9 %collective-permute-done.1 = bf16[2,8,64,128]{3,2,1,0:T(8,128)(2,1)S(1)} collective-permute-done((bf16[2,8,64,128]{3,2,1,0:T(8,128)(2,1)S(1)}, bf16[2,8,64,128]{3,2,1,0:T(8,128)(2,1)S(1)}, u32[]{:S(2)}, u32[]{:S(2)}) %collective-permute-start.1) | collective-permute-done | bytes 262176 | tf_op jit(solution)/shard_map/ppermute | solution.py:21
  16.4 0.9 fusion.6
  17.3 3.4 %collective-permute-start.2 = (bf16[12,2,64,128]{3,2,1,0:T(8,128)(2,1)}, bf16[12,2,64,128]{3,2,1,0:T(8,128)(2,1)S(1)}, u32[]{:S(2)}, u32[]{:S(2)}) collective-permute-start(bf16[12,2,64,128]{3,2,1,0:T(8,128)(2,1)} %get-tuple-element.67), channel_id=1, source_target_pairs={{0,8},{1,9},{2,10},{3,11},{4,12},{5,13},{6,14},{7,15},{16,24},{17,... | collective-permute-start | bytes 1179656 | tf_op jit(solution)/shard_map/ppermute | solution.py:21
  20.7 1.3 collective-permute-start.3
  22.0 0.0 copy-done.8
  22.1 0.7 copy.11.gain
  22.8 0.0 copy-done.6
  22.8 0.0 copy-done.7
  22.8 0.1 pad_maximum_fusion.1
  22.9 0.7 copy.12.w_t
  23.6 4.6 %collective-permute-done.2 = bf16[12,2,64,128]{3,2,1,0:T(8,128)(2,1)S(1)} collective-permute-done((bf16[12,2,64,128]{3,2,1,0:T(8,128)(2,1)}, bf16[12,2,64,128]{3,2,1,0:T(8,128)(2,1)S(1)}, u32[]{:S(2)}, u32[]{:S(2)}) %collective-permute-start.2) | collective-permute-done | bytes 393248 | tf_op jit(solution)/shard_map/ppermute | solution.py:21
  28.2 4.0 %collective-permute-done.3 = bf16[12,2,64,128]{3,2,1,0:T(8,128)(2,1)S(1)} collective-permute-done((bf16[12,2,64,128]{3,2,1,0:T(8,128)(2,1)}, bf16[12,2,64,128]{3,2,1,0:T(8,128)(2,1)S(1)}, u32[]{:S(2)}, u32[]{:S(2)}) %collective-permute-start.3) | collective-permute-done | bytes 393248 | tf_op jit(solution)/shard_map/ppermute | solution.py:21
  32.2 1.7 %pad_maximum_fusion.feat = bf16[12,12,64,128]{3,2,1,0:T(8,128)(2,1)} fusion(bf16[12,2,64,128]{3,2,1,0:T(8,128)(2,1)S(1)} %collective-permute-done.3, bf16[12,8,64,128]{3,2,1,0:T(8,128)(2,1)S(1)} %constant_dynamic-update-slice_fusion, bf16[12,2,64,128]{3,2,1,0:T(8,128)(2,1)S(1)} %collective-permute-done.2), kind=kLoop, calls=%fused_computation | loop fusion | flops 2359296 | bytes 4718592 | tf_op jit(solution)/shard_map/concatenate | solution.py:266
  34.0 43.9 %attend.1 = (bf16[8,8,64,128]{3,2,1,0:T(8,128)(2,1)}, bf16[8,8,64,128]{3,2,1,0:T(8,128)(2,1)}, bf16[12,12,128,128]{3,2,1,0:T(8,128)(2,1)}) custom-call(bf16[12,12,64,128]{3,2,1,0:T(8,128)(2,1)} %pad_maximum_fusion.feat, bf16[8,8,64,128]{3,2,1,0:T(8,128)(2,1)} %cot.3, f32[64,1]{1,0:T(8,128)} %copy.11.gain, bf16[192,64]{1,0:T(8,128)(2,1)} %copy.12.w_t, ...), custom_call_target="tpu_custom_call" | custom-call | tf_op jit(solution)/shard_map/attend/pallas_call | solution.py:166
  77.9 1.5 %fusion.4 = (bf16[12,2,128,128]{3,2,1,0:T(8,128)(2,1)S(1)}, bf16[12,2,128,128]{3,2,1,0:T(8,128)(2,1)S(1)}) fusion(bf16[12,12,128,128]{3,2,1,0:T(8,128)(2,1)} %get-tuple-element.59), kind=kLoop, calls=%fused_computation.14 | loop fusion | bytes 3145728 | tf_op jit(solution)/shard_map/slice | solution.py:271
  79.4 1.6 %collective-permute-start.4 = (bf16[12,2,128,128]{3,2,1,0:T(8,128)(2,1)S(1)}, bf16[12,2,128,128]{3,2,1,0:T(8,128)(2,1)S(1)}, u32[]{:S(2)}, u32[]{:S(2)}) collective-permute-start(bf16[12,2,128,128]{3,2,1,0:T(8,128)(2,1)S(1)} %get-tuple-element.64), channel_id=1, source_target_pairs={{0,8},{1,9},{2,10},{3,11},{4,12},{5,13},{6,14},{7,15},{16,24},{17,... | collective-permute-start | bytes 2359304 | tf_op jit(solution)/shard_map/ppermute | solution.py:21
  81.0 1.3 collective-permute-start.5
  82.3 2.1 %slice.164 = bf16[12,8,128,128]{3,2,1,0:T(8,128)(2,1)S(1)} slice(bf16[12,12,128,128]{3,2,1,0:T(8,128)(2,1)} %get-tuple-element.59), slice={[0:12], [2:10], [0:128], [0:128]} | slice | bytes 6291456 | tf_op jit(solution)/shard_map/slice | solution.py:275
  84.4 10.9 %collective-permute-done.4 = bf16[12,2,128,128]{3,2,1,0:T(8,128)(2,1)S(1)} collective-permute-done((bf16[12,2,128,128]{3,2,1,0:T(8,128)(2,1)S(1)}, bf16[12,2,128,128]{3,2,1,0:T(8,128)(2,1)S(1)}, u32[]{:S(2)}, u32[]{:S(2)}) %collective-permute-start.4) | collective-permute-done | bytes 786464 | tf_op jit(solution)/shard_map/ppermute | solution.py:21
  95.4 1.5 %add_dynamic-update-slice_fusion = bf16[12,8,128,128]{3,2,1,0:T(8,128)(2,1)S(1)} fusion(bf16[12,8,128,128]{3,2,1,0:T(8,128)(2,1)S(1)} %slice.164, bf16[12,2,128,128]{3,2,1,0:T(8,128)(2,1)S(1)} %collective-permute-done.4, bf16[12,12,128,128]{3,2,1,0:T(8,128)(2,1)} %get-tuple-element.59), kind=kLoop, calls=%fused_computation.3 | loop fusion | flops 1572864 | bytes 2359296 | tf_op jit(solution)/shard_map/scatter-add | solution.py:278
  96.9 2.7 %collective-permute-done.5 = bf16[12,2,128,128]{3,2,1,0:T(8,128)(2,1)S(1)} collective-permute-done((bf16[12,2,128,128]{3,2,1,0:T(8,128)(2,1)S(1)}, bf16[12,2,128,128]{3,2,1,0:T(8,128)(2,1)S(1)}, u32[]{:S(2)}, u32[]{:S(2)}) %collective-permute-start.5) | collective-permute-done | bytes 786464 | tf_op jit(solution)/shard_map/ppermute | solution.py:21
  99.5 0.4 fusion
  99.9 0.1 fusion.5
  100.0 1.5 %collective-permute-start.6 = (bf16[2,8,128,128]{3,2,1,0:T(8,128)(2,1)S(1)}, bf16[2,8,128,128]{3,2,1,0:T(8,128)(2,1)S(1)}, u32[]{:S(2)}, u32[]{:S(2)}) collective-permute-start(bf16[2,8,128,128]{3,2,1,0:T(8,128)(2,1)S(1)} %get-tuple-element.66), channel_id=1, source_target_pairs={{0,16},{1,17},{2,18},{3,19},{4,20},{5,21},{6,22},{7,23},{8,24},{9,... | collective-permute-start | bytes 1572872 | tf_op jit(solution)/shard_map/ppermute | solution.py:21
  101.5 1.3 collective-permute-start.7
  102.8 0.0 copy-start.4
  102.8 0.0 copy-start.5
  102.8 0.1 slice.181
  103.0 0.0 copy-start.1
  103.0 0.0 copy-start.2
  103.0 0.0 copy-start.3
  103.0 6.2 %collective-permute-done.6 = bf16[2,8,128,128]{3,2,1,0:T(8,128)(2,1)S(1)} collective-permute-done((bf16[2,8,128,128]{3,2,1,0:T(8,128)(2,1)S(1)}, bf16[2,8,128,128]{3,2,1,0:T(8,128)(2,1)S(1)}, u32[]{:S(2)}, u32[]{:S(2)}) %collective-permute-start.6) | collective-permute-done | bytes 524320 | tf_op jit(solution)/shard_map/ppermute | solution.py:21
  109.2 0.2 fusion.2
  109.4 4.0 %collective-permute-done.7 = bf16[2,8,128,128]{3,2,1,0:T(8,128)(2,1)S(1)} collective-permute-done((bf16[2,8,128,128]{3,2,1,0:T(8,128)(2,1)S(1)}, bf16[2,8,128,128]{3,2,1,0:T(8,128)(2,1)S(1)}, u32[]{:S(2)}, u32[]{:S(2)}) %collective-permute-start.7) | collective-permute-done | bytes 524320 | tf_op jit(solution)/shard_map/ppermute | solution.py:21
  113.3 0.3 fusion.1.dkv
  113.6 0.0 copy-done.4
  113.6 0.0 copy-done.5
  113.6 0.0 copy-done.1
  113.6 0.0 copy-done.2
  113.7 0.0 copy-done.3
  113.7 6.8 %back.1 = (bf16[8,8,64,128]{3,2,1,0:T(8,128)(2,1)}, f32[72,256]{1,0:T(8,128)S(1)}) custom-call(bf16[8,8,64,128]{3,2,1,0:T(8,128)(2,1)S(1)} %copy-done, bf16[8,8,64,128]{3,2,1,0:T(8,128)(2,1)S(1)} %copy-done.1, bf16[8,8,64,128]{3,2,1,0:T(8,128)(2,1)S(1)} %copy-done.2, bf16[8,8,128,128]{3,2,1,0:T(8,128)(2,1)S(1)} %fusion.1.dkv, ...), custom_call_target="tpu_custom_call" | custom-call | tf_op jit(solution)/shard_map/back/pallas_call | solution.py:237
  120.5 0.0 collective-permute-start.8
  120.5 1.3 collective-permute-done.8
  121.7 1.6 %collective-permute-start.9 = (f32[72,256]{1,0:T(8,128)S(1)}, f32[72,256]{1,0:T(8,128)S(1)}, u32[]{:S(2)}, u32[]{:S(2)}) collective-permute-start(f32[72,256]{1,0:T(8,128)S(1)} %add.47), channel_id=1, source_target_pairs={{0,2},{1,3},{2,0},{3,1},{4,6},{5,7},{6,4},{7,5},{8,10},{9,11},{10,... | collective-permute-start | bytes 221192 | tf_op jit(solution)/shard_map/ppermute | solution.py:257
  123.4 2.8 %collective-permute-done.9 = f32[72,256]{1,0:T(8,128)S(1)} collective-permute-done((f32[72,256]{1,0:T(8,128)S(1)}, f32[72,256]{1,0:T(8,128)S(1)}, u32[]{:S(2)}, u32[]{:S(2)}) %collective-permute-start.9) | collective-permute-done | bytes 73760 | tf_op jit(solution)/shard_map/ppermute | solution.py:257
  126.2 2.6 %collective-permute-start.10 = (f32[72,256]{1,0:T(8,128)S(1)}, f32[72,256]{1,0:T(8,128)S(1)}, u32[]{:S(2)}, u32[]{:S(2)}) collective-permute-start(f32[72,256]{1,0:T(8,128)S(1)} %add.48), channel_id=1, source_target_pairs={{0,4},{1,5},{2,6},{3,7},{4,0},{5,1},{6,2},{7,3},{8,12},{9,13},{10,... | collective-permute-start | bytes 221192 | tf_op jit(solution)/shard_map/ppermute | solution.py:257
  128.8 2.7 %collective-permute-done.10 = f32[72,256]{1,0:T(8,128)S(1)} collective-permute-done((f32[72,256]{1,0:T(8,128)S(1)}, f32[72,256]{1,0:T(8,128)S(1)}, u32[]{:S(2)}, u32[]{:S(2)}) %collective-permute-start.10) | collective-permute-done | bytes 73760 | tf_op jit(solution)/shard_map/ppermute | solution.py:257
  131.5 0.2 collective-permute-start.11
  131.7 4.3 %collective-permute-done.11 = f32[72,256]{1,0:T(8,128)S(1)} collective-permute-done((f32[72,256]{1,0:T(8,128)S(1)}, f32[72,256]{1,0:T(8,128)S(1)}, u32[]{:S(2)}, u32[]{:S(2)}) %collective-permute-start.11) | collective-permute-done | bytes 73760 | tf_op jit(solution)/shard_map/ppermute | solution.py:257
  135.9 0.1 collective-permute-start.12
  136.0 4.3 %collective-permute-done.12 = f32[72,256]{1,0:T(8,128)S(1)} collective-permute-done((f32[72,256]{1,0:T(8,128)S(1)}, f32[72,256]{1,0:T(8,128)S(1)}, u32[]{:S(2)}, u32[]{:S(2)}) %collective-permute-start.12) | collective-permute-done | bytes 73760 | tf_op jit(solution)/shard_map/ppermute | solution.py:257
  140.4 0.5 slice_bitcast_fusion
  140.9 0.7 slice.187
  141.6 0.7 fusion.8
  (7 shorter events, 0.1 us)
Async XLA Ops:
  0.6 11.6 %copy-start = (bf16[8,8,64,128]{3,2,1,0:T(8,128)(2,1)S(1)}, bf16[8,8,64,128]{3,2,1,0:T(8,128)(2,1)}, u32[]{:S(2)}) copy-start(bf16[8,8,64,128]{3,2,1,0:T(8,128)(2,1)} %feat.1) | copy-start | bytes 3145732
  1.8 10.4 %collective-permute-start = (bf16[2,8,64,128]{3,2,1,0:T(8,128)(2,1)S(1)}, bf16[2,8,64,128]{3,2,1,0:T(8,128)(2,1)S(1)}, u32[]{:S(2)}, u32[]{:S(2)}) collective-permute-start(bf16[2,8,64,128]{3,2,1,0:T(8,128)(2,1)S(1)} %get-tuple-element.70), channel_id=1, source_target_pairs={{0,16},{1,17},{2,18},{3,19},{4,20},{5,21},{6,22},{7,23},{8,24},{9,... | collective-permute-start | bytes 786440 | tf_op jit(solution)/shard_map/ppermute | solution.py:21
  6.7 9.7 %collective-permute-start.1 = (bf16[2,8,64,128]{3,2,1,0:T(8,128)(2,1)S(1)}, bf16[2,8,64,128]{3,2,1,0:T(8,128)(2,1)S(1)}, u32[]{:S(2)}, u32[]{:S(2)}) collective-permute-start(bf16[2,8,64,128]{3,2,1,0:T(8,128)(2,1)S(1)} %get-tuple-element.69), channel_id=1, source_target_pairs={{16,0},{17,1},{18,2},{19,3},{20,4},{21,5},{22,6},{23,7},{24,8},{25... | collective-permute-start | bytes 786440 | tf_op jit(solution)/shard_map/ppermute | solution.py:21
  12.3 9.8 %copy-start.8 = (f32[64]{0:T(128)S(1)}, f32[64]{0:T(128)}, u32[]{:S(2)}) copy-start(f32[64]{0:T(128)} %param.16) | copy-start | bytes 772
  12.3 10.5 %copy-start.6 = (bf16[64,128]{1,0:T(8,128)(2,1)S(1)}, bf16[64,128]{1,0:T(8,128)(2,1)}, u32[]{:S(2)}) copy-start(bf16[64,128]{1,0:T(8,128)(2,1)} %param.18) | copy-start | bytes 49156
  12.3 10.5 %copy-start.7 = (bf16[64,64]{1,0:T(8,128)(2,1)S(1)}, bf16[64,64]{1,0:T(8,128)(2,1)}, u32[]{:S(2)}) copy-start(bf16[64,64]{1,0:T(8,128)(2,1)} %param.17) | copy-start | bytes 24580
  17.3 10.9 %collective-permute-start.2 = (bf16[12,2,64,128]{3,2,1,0:T(8,128)(2,1)}, bf16[12,2,64,128]{3,2,1,0:T(8,128)(2,1)S(1)}, u32[]{:S(2)}, u32[]{:S(2)}) collective-permute-start(bf16[12,2,64,128]{3,2,1,0:T(8,128)(2,1)} %get-tuple-element.67), channel_id=1, source_target_pairs={{0,8},{1,9},{2,10},{3,11},{4,12},{5,13},{6,14},{7,15},{16,24},{17,... | collective-permute-start | bytes 1179656 | tf_op jit(solution)/shard_map/ppermute | solution.py:21
  20.7 11.5 %collective-permute-start.3 = (bf16[12,2,64,128]{3,2,1,0:T(8,128)(2,1)}, bf16[12,2,64,128]{3,2,1,0:T(8,128)(2,1)S(1)}, u32[]{:S(2)}, u32[]{:S(2)}) collective-permute-start(bf16[12,2,64,128]{3,2,1,0:T(8,128)(2,1)} %get-tuple-element.68), channel_id=1, source_target_pairs={{8,0},{9,1},{10,2},{11,3},{12,4},{13,5},{14,6},{15,7},{24,16},{25,... | collective-permute-start | bytes 1179656 | tf_op jit(solution)/shard_map/ppermute | solution.py:21
  79.4 16.0 %collective-permute-start.4 = (bf16[12,2,128,128]{3,2,1,0:T(8,128)(2,1)S(1)}, bf16[12,2,128,128]{3,2,1,0:T(8,128)(2,1)S(1)}, u32[]{:S(2)}, u32[]{:S(2)}) collective-permute-start(bf16[12,2,128,128]{3,2,1,0:T(8,128)(2,1)S(1)} %get-tuple-element.64), channel_id=1, source_target_pairs={{0,8},{1,9},{2,10},{3,11},{4,12},{5,13},{6,14},{7,15},{16,24},{17,... | collective-permute-start | bytes 2359304 | tf_op jit(solution)/shard_map/ppermute | solution.py:21
  81.0 18.5 %collective-permute-start.5 = (bf16[12,2,128,128]{3,2,1,0:T(8,128)(2,1)S(1)}, bf16[12,2,128,128]{3,2,1,0:T(8,128)(2,1)S(1)}, u32[]{:S(2)}, u32[]{:S(2)}) collective-permute-start(bf16[12,2,128,128]{3,2,1,0:T(8,128)(2,1)S(1)} %get-tuple-element.63), channel_id=1, source_target_pairs={{8,0},{9,1},{10,2},{11,3},{12,4},{13,5},{14,6},{15,7},{24,16},{25,... | collective-permute-start | bytes 2359304 | tf_op jit(solution)/shard_map/ppermute | solution.py:21
  100.0 9.2 %collective-permute-start.6 = (bf16[2,8,128,128]{3,2,1,0:T(8,128)(2,1)S(1)}, bf16[2,8,128,128]{3,2,1,0:T(8,128)(2,1)S(1)}, u32[]{:S(2)}, u32[]{:S(2)}) collective-permute-start(bf16[2,8,128,128]{3,2,1,0:T(8,128)(2,1)S(1)} %get-tuple-element.66), channel_id=1, source_target_pairs={{0,16},{1,17},{2,18},{3,19},{4,20},{5,21},{6,22},{7,23},{8,24},{9,... | collective-permute-start | bytes 1572872 | tf_op jit(solution)/shard_map/ppermute | solution.py:21
  101.5 11.8 %collective-permute-start.7 = (bf16[2,8,128,128]{3,2,1,0:T(8,128)(2,1)S(1)}, bf16[2,8,128,128]{3,2,1,0:T(8,128)(2,1)S(1)}, u32[]{:S(2)}, u32[]{:S(2)}) collective-permute-start(bf16[2,8,128,128]{3,2,1,0:T(8,128)(2,1)S(1)} %get-tuple-element.65), channel_id=1, source_target_pairs={{16,0},{17,1},{18,2},{19,3},{20,4},{21,5},{22,6},{23,7},{24,8},{25... | collective-permute-start | bytes 1572872 | tf_op jit(solution)/shard_map/ppermute | solution.py:21
  102.8 10.8 %copy-start.4 = (bf16[192,64]{1,0:T(8,128)(2,1)S(1)}, bf16[192,64]{1,0:T(8,128)(2,1)}, u32[]{:S(2)}) copy-start(bf16[192,64]{1,0:T(8,128)(2,1)} %copy.12.w_t) | copy-start | bytes 73732
  102.8 10.8 %copy-start.5 = (f32[64,1]{1,0:T(8,128)S(1)}, f32[64,1]{1,0:T(8,128)}, u32[]{:S(2)}) copy-start(f32[64,1]{1,0:T(8,128)} %copy.11.gain) | copy-start | bytes 772
  103.0 10.7 %copy-start.1 = (bf16[8,8,64,128]{3,2,1,0:T(8,128)(2,1)S(1)}, bf16[8,8,64,128]{3,2,1,0:T(8,128)(2,1)}, u32[]{:S(2)}) copy-start(bf16[8,8,64,128]{3,2,1,0:T(8,128)(2,1)} %cot.3) | copy-start | bytes 3145732
  103.0 10.7 %copy-start.2 = (bf16[8,8,64,128]{3,2,1,0:T(8,128)(2,1)S(1)}, bf16[8,8,64,128]{3,2,1,0:T(8,128)(2,1)}, u32[]{:S(2)}) copy-start(bf16[8,8,64,128]{3,2,1,0:T(8,128)(2,1)} %get-tuple-element.58.dq) | copy-start | bytes 3145732
  103.0 10.7 %copy-start.3 = (bf16[8,8,64,128]{3,2,1,0:T(8,128)(2,1)S(1)}, bf16[8,8,64,128]{3,2,1,0:T(8,128)(2,1)}, u32[]{:S(2)}) copy-start(bf16[8,8,64,128]{3,2,1,0:T(8,128)(2,1)} %get-tuple-element.60.att) | copy-start | bytes 3145732
  120.5 1.3 collective-permute-start.8
  121.7 4.4 %collective-permute-start.9 = (f32[72,256]{1,0:T(8,128)S(1)}, f32[72,256]{1,0:T(8,128)S(1)}, u32[]{:S(2)}, u32[]{:S(2)}) collective-permute-start(f32[72,256]{1,0:T(8,128)S(1)} %add.47), channel_id=1, source_target_pairs={{0,2},{1,3},{2,0},{3,1},{4,6},{5,7},{6,4},{7,5},{8,10},{9,11},{10,... | collective-permute-start | bytes 221192 | tf_op jit(solution)/shard_map/ppermute | solution.py:257
  126.2 5.3 %collective-permute-start.10 = (f32[72,256]{1,0:T(8,128)S(1)}, f32[72,256]{1,0:T(8,128)S(1)}, u32[]{:S(2)}, u32[]{:S(2)}) collective-permute-start(f32[72,256]{1,0:T(8,128)S(1)} %add.48), channel_id=1, source_target_pairs={{0,4},{1,5},{2,6},{3,7},{4,0},{5,1},{6,2},{7,3},{8,12},{9,13},{10,... | collective-permute-start | bytes 221192 | tf_op jit(solution)/shard_map/ppermute | solution.py:257
  131.5 4.4 %collective-permute-start.11 = (f32[72,256]{1,0:T(8,128)S(1)}, f32[72,256]{1,0:T(8,128)S(1)}, u32[]{:S(2)}, u32[]{:S(2)}) collective-permute-start(f32[72,256]{1,0:T(8,128)S(1)} %add.49), channel_id=1, source_target_pairs={{0,8},{8,0},{1,9},{9,1},{2,10},{10,2},{3,11},{11,3},{4,12},{12,4},... | collective-permute-start | bytes 221192 | tf_op jit(solution)/shard_map/ppermute | solution.py:257
  135.9 4.4 %collective-permute-start.12 = (f32[72,256]{1,0:T(8,128)S(1)}, f32[72,256]{1,0:T(8,128)S(1)}, u32[]{:S(2)}, u32[]{:S(2)}) collective-permute-start(f32[72,256]{1,0:T(8,128)S(1)} %add.50), channel_id=1, source_target_pairs={{0,16},{16,0},{1,17},{17,1},{2,18},{18,2},{3,19},{19,3},{4,20},{20... | collective-permute-start | bytes 221192 | tf_op jit(solution)/shard_map/ppermute | solution.py:257

commit v3 on v2

--- a/solution.py
+++ b/solution.py
@@ -19,6 +19,15 @@
     count = lax.axis_size(axis)
     pairs = [(i, i + 1) if up else (i + 1, i) for i in range(count - 1)]
     return lax.ppermute(block, axis, pairs)
+
+
+def exchange(to_before, to_after, axis):
+    if lax.axis_size(axis) != 2:
+        return shift(to_after, axis, True), shift(to_before, axis, False)
+    first = lax.axis_index(axis) == 0
+    came = lax.ppermute(jnp.where(first, to_after, to_before), axis, [(0, 1), (1, 0)])
+    none = jnp.zeros_like(came)
+    return jnp.where(first, none, came), jnp.where(first, came, none)
 
 
 def lanes(ref, row, cols):
@@ -261,8 +270,9 @@
 
 def extended(block, axis, dim):
     length = block.shape[dim]
-    before = shift(lax.slice_in_dim(block, length - REACH, length, axis=dim), axis, True)
-    after = shift(lax.slice_in_dim(block, 0, REACH, axis=dim), axis, False)
+    leading = lax.slice_in_dim(block, 0, REACH, axis=dim)
+    last = lax.slice_in_dim(block, length - REACH, length, axis=dim)
+    before, after = exchange(leading, last, axis)
     return jnp.concatenate([before, block, after], axis=dim)
 
 
@@ -270,8 +280,7 @@
     length = block.shape[dim]
     to_before = lax.slice_in_dim(block, 0, REACH, axis=dim)
     to_after = lax.slice_in_dim(block, length - REACH, length, axis=dim)
-    from_after = shift(to_before, axis, False)
-    from_before = shift(to_after, axis, True)
+    from_before, from_after = exchange(to_before, to_after, axis)
     own = lax.slice_in_dim(block, REACH, length - REACH, axis=dim)
     first = (slice(None),) * dim + (slice(0, REACH),)
     last = (slice(None),) * dim + (slice(own.shape[dim] - REACH, None),)

time: 143 us -> 131 us (0.916)
  starting transfers between devices: 21 us -> 10.4 us
  other arithmetic: 4.17 us -> 8.13 us
  local copies, waits for them, and re-layouts: 9.58 us -> 5.62 us
    ppermute x8 -> x4, starting transfers between devices: 16.5 us -> 7.43 us  [exchange(): lax.ppermute(jnp.where(first, to_after, to_before), axis, [(0, 1), (1, 0)])]
    select_n x0 -> x6, other arithmetic: none -> 3.88 us  [the longest x4 3.79 us: exchange(): jnp.where(first, to_after, to_before)]
    slice x4 -> x0, local copies, waits for them, and re-layouts: 3.71 us -> none  [the longest x2 1.61 us: folded(): to_before = lax.slice_in_dim(block, 0, REACH, axis=dim)]
    ppermute x8 -> x4, waiting for transfers between devices: 40.5 us -> 37.6 us  [exchange(): lax.ppermute(jnp.where(first, to_after, to_before), axis, [(0, 1), (1, 0)])]
    ppermute x5, waiting for transfers between devices: 15.3 us -> 17.6 us  [summed(): lax.ppermute(block, axis, [(i, i ^ hop) for i in range(count)])]
    ppermute x5, starting transfers between devices: 4.48 us -> 2.99 us  [summed(): lax.ppermute(block, axis, [(i, i ^ hop) for i in range(count)])]
  transfers between devices with their start and end apart: 13 -> 9, of which waited for: 13 -> 9; matrix products, arithmetic and copies ran while one was open for 4% -> 3% of each run, Pallas kernels for 0% -> 0%
where the time goes in v3:
time: 131 us
  waiting for transfers between devices  55.3 us (42%)
  Pallas kernels  50.7 us (39%)
  starting transfers between devices  10.4 us (8%)
  other arithmetic  8.13 us (6%)
  local copies, waits for them, and re-layouts  5.62 us (4%)
    pallas_call x1, Pallas kernels, attend(): pl.pallas_call(attend_kernel, out_shape=(jax.ShapeDtypeStruct(cot.shape,...  43.9 us
    ppermute x4, waiting for transfers between devices, exchange(): lax.ppermute(jnp.where(first, to_after, to_before), axis, [(0, 1), (1, 0)])  37.6 us
    ppermute x5, waiting for transfers between devices, summed(): lax.ppermute(block, axis, [(i, i ^ hop) for i in range(count)])  17.6 us
    ppermute x4, starting transfers between devices, exchange(): lax.ppermute(jnp.where(first, to_after, to_before), axis, [(0, 1), (1, 0)])  7.43 us
    pallas_call x1, Pallas kernels, back(): pl.pallas_call(functools.partial(back_kernel, factor), grid=(rows,), out_...  6.78 us
    select_n x4, other arithmetic, exchange(): jnp.where(first, to_after, to_before)  3.79 us
    ppermute x5, starting transfers between devices, summed(): lax.ppermute(block, axis, [(i, i ^ hop) for i in range(count)])  2.99 us
  transfers between devices with their start and end apart: 9, of which 9 were waited for; matrix products, arithmetic and copies ran while one was open for 3% of the time, Pallas kernels for 0%

profile of v3, /device:TPU:0, one launch (start us, length us, event | category | flops | bytes accessed | tf_op | source)
XLA Modules:
  0.0 131.0 jit_solution(15642583146905003761)
XLA Ops:
  0.6 0.0 copy-start.8
  0.6 0.0 copy-start.6
  0.7 0.0 copy-start.7
  0.7 0.0 copy-start
  0.7 1.1 slice_select_fusion.2
  1.8 3.0 %collective-permute-start = (bf16[2,8,64,128]{3,2,1,0:T(8,128)(2,1)S(1)}, bf16[2,8,64,128]{3,2,1,0:T(8,128)(2,1)S(1)}, u32[]{:S(2)}, u32[]{:S(2)}) collective-permute-start(bf16[2,8,64,128]{3,2,1,0:T(8,128)(2,1)S(1)} %slice_select_fusion.2), channel_id=1, source_target_pairs={{0,16},{16,0},{1,17},{17,1},{2,18},{18,2},{3,19},{19,3},{4,20},{20... | collective-permute-start | bytes 786440 | tf_op jit(solution)/shard_map/ppermute | solution.py:28
  4.9 6.3 %collective-permute-done = bf16[2,8,64,128]{3,2,1,0:T(8,128)(2,1)S(1)} collective-permute-done((bf16[2,8,64,128]{3,2,1,0:T(8,128)(2,1)S(1)}, bf16[2,8,64,128]{3,2,1,0:T(8,128)(2,1)S(1)}, u32[]{:S(2)}, u32[]{:S(2)}) %collective-permute-start) | collective-permute-done | bytes 262176 | tf_op jit(solution)/shard_map/ppermute | solution.py:28
  11.2 1.1 fusion.3
  12.3 1.8 %collective-permute-start.1 = (bf16[12,2,64,128]{3,2,1,0:T(8,128)(2,1)S(1)}, bf16[12,2,64,128]{3,2,1,0:T(8,128)(2,1)S(1)}, u32[]{:S(2)}, u32[]{:S(2)}) collective-permute-start(bf16[12,2,64,128]{3,2,1,0:T(8,128)(2,1)S(1)} %fusion.3), channel_id=1, source_target_pairs={{0,8},{8,0},{1,9},{9,1},{2,10},{10,2},{3,11},{11,3},{4,12},{12,4},... | collective-permute-start | bytes 1179656 | tf_op jit(solution)/shard_map/ppermute | solution.py:28
  14.1 0.0 copy-done.8
  14.1 0.7 copy.11.gain
  14.8 0.0 copy-done.6
  14.8 0.0 copy-done.7
  14.8 0.1 pad_maximum_fusion.3
  14.9 0.7 copy.12.w_t
  15.6 7.1 %collective-permute-done.1 = bf16[12,2,64,128]{3,2,1,0:T(8,128)(2,1)S(1)} collective-permute-done((bf16[12,2,64,128]{3,2,1,0:T(8,128)(2,1)S(1)}, bf16[12,2,64,128]{3,2,1,0:T(8,128)(2,1)S(1)}, u32[]{:S(2)}, u32[]{:S(2)}) %collective-permute-start.1) | collective-permute-done | bytes 393248 | tf_op jit(solution)/shard_map/ppermute | solution.py:28
  22.7 0.1 broadcast_select_fusion.1
  22.8 0.0 copy-done
  22.8 1.7 %pad_maximum_fusion.feat = bf16[12,12,64,128]{3,2,1,0:T(8,128)(2,1)} fusion(bf16[12,2,64,128]{3,2,1,0:T(8,128)(2,1)S(1)} %get-tuple-element.64, bf16[2,8,64,128]{3,2,1,0:T(8,128)(2,1)S(1)} %get-tuple-element.66, bf16[8,8,64,128]{3,2,1,0:T(8,128)(2,1)S(1)} %copy-done, bf16[2,8,64,128]{3,2,1,0:T(8,128)(2,1)S(1)} %get-tuple-element.65, ...), kind=kLoop, calls=%fused_computation | loop fusion | flops 4718592 | bytes 4718592 | tf_op jit(solution)/shard_map/concatenate | solution.py:276
  24.5 43.9 %attend.1 = (bf16[8,8,64,128]{3,2,1,0:T(8,128)(2,1)}, bf16[8,8,64,128]{3,2,1,0:T(8,128)(2,1)}, bf16[12,12,128,128]{3,2,1,0:T(8,128)(2,1)}) custom-call(bf16[12,12,64,128]{3,2,1,0:T(8,128)(2,1)} %pad_maximum_fusion.feat, bf16[8,8,64,128]{3,2,1,0:T(8,128)(2,1)} %cot.3, f32[64,1]{1,0:T(8,128)} %copy.11.gain, bf16[192,64]{1,0:T(8,128)(2,1)} %copy.12.w_t, ...), custom_call_target="tpu_custom_call" | custom-call | tf_op jit(solution)/shard_map/attend/pallas_call | solution.py:175
  68.4 1.5 %slice_select_fusion = bf16[12,2,128,128]{3,2,1,0:T(8,128)(2,1)S(1)} fusion(bf16[12,12,128,128]{3,2,1,0:T(8,128)(2,1)} %get-tuple-element.59, pred[]{:T(512)S(6)} %eq.8), kind=kLoop, calls=%fused_computation.4 | loop fusion | flops 393216 | bytes 2359297 | tf_op jit(solution)/shard_map/jit(_where)/select_n | solution.py:28
  69.9 1.5 %collective-permute-start.2 = (bf16[12,2,128,128]{3,2,1,0:T(8,128)(2,1)S(1)}, bf16[12,2,128,128]{3,2,1,0:T(8,128)(2,1)S(1)}, u32[]{:S(2)}, u32[]{:S(2)}) collective-permute-start(bf16[12,2,128,128]{3,2,1,0:T(8,128)(2,1)S(1)} %slice_select_fusion), channel_id=1, source_target_pairs={{0,8},{8,0},{1,9},{9,1},{2,10},{10,2},{3,11},{11,3},{4,12},{12,4},... | collective-permute-start | bytes 2359304 | tf_op jit(solution)/shard_map/ppermute | solution.py:28
  71.3 2.1 %slice.164 = bf16[12,8,128,128]{3,2,1,0:T(8,128)(2,1)S(1)} slice(bf16[12,12,128,128]{3,2,1,0:T(8,128)(2,1)} %get-tuple-element.59), slice={[0:12], [2:10], [0:128], [0:128]} | slice | bytes 6291456 | tf_op jit(solution)/shard_map/slice | solution.py:284
  73.4 14.3 %collective-permute-done.2 = bf16[12,2,128,128]{3,2,1,0:T(8,128)(2,1)S(1)} collective-permute-done((bf16[12,2,128,128]{3,2,1,0:T(8,128)(2,1)S(1)}, bf16[12,2,128,128]{3,2,1,0:T(8,128)(2,1)S(1)}, u32[]{:S(2)}, u32[]{:S(2)}) %collective-permute-start.2) | collective-permute-done | bytes 786464 | tf_op jit(solution)/shard_map/ppermute | solution.py:28
  87.7 1.5 %add_dynamic-update-slice_fusion = bf16[12,8,128,128]{3,2,1,0:T(8,128)(2,1)S(1)} fusion(bf16[12,8,128,128]{3,2,1,0:T(8,128)(2,1)S(1)} %slice.164, bf16[12,2,128,128]{3,2,1,0:T(8,128)(2,1)S(1)} %collective-permute-done.2, bf16[12,12,128,128]{3,2,1,0:T(8,128)(2,1)} %get-tuple-element.59, pred[]{:T(512)S(6)} %eq.8), kind=kLoop, calls=%fused_computation.3 | loop fusion | flops 1966080 | bytes 2359297 | tf_op jit(solution)/shard_map/scatter-add | solution.py:287
  89.2 0.4 fusion
  89.6 0.1 slice_select_fusion.1
  89.7 1.2 collective-permute-start.3
  90.9 0.0 copy-start.4
  90.9 0.0 copy-start.5
  90.9 0.1 slice.179
  91.0 0.0 copy-start.1
  91.0 0.0 copy-start.2
  91.0 0.0 copy-start.3
  91.0 10.0 %collective-permute-done.3 = bf16[2,8,128,128]{3,2,1,0:T(8,128)(2,1)S(1)} collective-permute-done((bf16[2,8,128,128]{3,2,1,0:T(8,128)(2,1)S(1)}, bf16[2,8,128,128]{3,2,1,0:T(8,128)(2,1)S(1)}, u32[]{:S(2)}, u32[]{:S(2)}) %collective-permute-start.3) | collective-permute-done | bytes 524320 | tf_op jit(solution)/shard_map/ppermute | solution.py:28
  101.0 0.2 fusion.2
  101.2 0.3 fusion.1.dkv
  101.5 0.0 copy-done.4
  101.6 0.0 copy-done.5
  101.6 0.0 copy-done.1
  101.6 0.0 copy-done.2
  101.6 0.0 copy-done.3
  101.6 6.8 %back.1 = (bf16[8,8,64,128]{3,2,1,0:T(8,128)(2,1)}, f32[72,256]{1,0:T(8,128)S(1)}) custom-call(bf16[8,8,64,128]{3,2,1,0:T(8,128)(2,1)S(1)} %copy-done, bf16[8,8,64,128]{3,2,1,0:T(8,128)(2,1)S(1)} %copy-done.1, bf16[8,8,64,128]{3,2,1,0:T(8,128)(2,1)S(1)} %copy-done.2, bf16[8,8,128,128]{3,2,1,0:T(8,128)(2,1)S(1)} %fusion.1.dkv, ...), custom_call_target="tpu_custom_call" | custom-call | tf_op jit(solution)/shard_map/back/pallas_call | solution.py:246
  108.4 0.0 collective-permute-start.4
  108.4 1.3 collective-permute-done.4
  109.7 0.9 collective-permute-start.5
  110.6 3.5 %collective-permute-done.5 = f32[72,256]{1,0:T(8,128)S(1)} collective-permute-done((f32[72,256]{1,0:T(8,128)S(1)}, f32[72,256]{1,0:T(8,128)S(1)}, u32[]{:S(2)}, u32[]{:S(2)}) %collective-permute-start.5) | collective-permute-done | bytes 73760 | tf_op jit(solution)/shard_map/ppermute | solution.py:266
  114.1 1.9 %collective-permute-start.6 = (f32[72,256]{1,0:T(8,128)S(1)}, f32[72,256]{1,0:T(8,128)S(1)}, u32[]{:S(2)}, u32[]{:S(2)}) collective-permute-start(f32[72,256]{1,0:T(8,128)S(1)} %add.48), channel_id=1, source_target_pairs={{0,4},{1,5},{2,6},{3,7},{4,0},{5,1},{6,2},{7,3},{8,12},{9,13},{10,... | collective-permute-start | bytes 221192 | tf_op jit(solution)/shard_map/ppermute | solution.py:266
  116.0 4.2 %collective-permute-done.6 = f32[72,256]{1,0:T(8,128)S(1)} collective-permute-done((f32[72,256]{1,0:T(8,128)S(1)}, f32[72,256]{1,0:T(8,128)S(1)}, u32[]{:S(2)}, u32[]{:S(2)}) %collective-permute-start.6) | collective-permute-done | bytes 73760 | tf_op jit(solution)/shard_map/ppermute | solution.py:266
  120.2 0.1 collective-permute-start.7
  120.3 4.3 %collective-permute-done.7 = f32[72,256]{1,0:T(8,128)S(1)} collective-permute-done((f32[72,256]{1,0:T(8,128)S(1)}, f32[72,256]{1,0:T(8,128)S(1)}, u32[]{:S(2)}, u32[]{:S(2)}) %collective-permute-start.7) | collective-permute-done | bytes 73760 | tf_op jit(solution)/shard_map/ppermute | solution.py:266
  124.6 0.1 collective-permute-start.8
  124.7 4.3 %collective-permute-done.8 = f32[72,256]{1,0:T(8,128)S(1)} collective-permute-done((f32[72,256]{1,0:T(8,128)S(1)}, f32[72,256]{1,0:T(8,128)S(1)}, u32[]{:S(2)}, u32[]{:S(2)}) %collective-permute-start.8) | collective-permute-done | bytes 73760 | tf_op jit(solution)/shard_map/ppermute | solution.py:266
  129.1 0.5 slice_bitcast_fusion
  129.6 0.7 slice.185
  130.3 0.7 fusion.5
  (6 shorter events, 0.1 us)
Async XLA Ops:
  0.6 13.5 %copy-start.8 = (f32[64]{0:T(128)S(1)}, f32[64]{0:T(128)}, u32[]{:S(2)}) copy-start(f32[64]{0:T(128)} %param.16) | copy-start | bytes 772
  0.6 14.2 %copy-start.6 = (bf16[64,128]{1,0:T(8,128)(2,1)S(1)}, bf16[64,128]{1,0:T(8,128)(2,1)}, u32[]{:S(2)}) copy-start(bf16[64,128]{1,0:T(8,128)(2,1)} %param.18) | copy-start | bytes 49156
  0.7 14.2 %copy-start.7 = (bf16[64,64]{1,0:T(8,128)(2,1)S(1)}, bf16[64,64]{1,0:T(8,128)(2,1)}, u32[]{:S(2)}) copy-start(bf16[64,64]{1,0:T(8,128)(2,1)} %param.17) | copy-start | bytes 24580
  0.7 22.1 %copy-start = (bf16[8,8,64,128]{3,2,1,0:T(8,128)(2,1)S(1)}, bf16[8,8,64,128]{3,2,1,0:T(8,128)(2,1)}, u32[]{:S(2)}) copy-start(bf16[8,8,64,128]{3,2,1,0:T(8,128)(2,1)} %feat.1) | copy-start | bytes 3145732
  1.8 9.3 %collective-permute-start = (bf16[2,8,64,128]{3,2,1,0:T(8,128)(2,1)S(1)}, bf16[2,8,64,128]{3,2,1,0:T(8,128)(2,1)S(1)}, u32[]{:S(2)}, u32[]{:S(2)}) collective-permute-start(bf16[2,8,64,128]{3,2,1,0:T(8,128)(2,1)S(1)} %slice_select_fusion.2), channel_id=1, source_target_pairs={{0,16},{16,0},{1,17},{17,1},{2,18},{18,2},{3,19},{19,3},{4,20},{20... | collective-permute-start | bytes 786440 | tf_op jit(solution)/shard_map/ppermute | solution.py:28
  12.3 10.4 %collective-permute-start.1 = (bf16[12,2,64,128]{3,2,1,0:T(8,128)(2,1)S(1)}, bf16[12,2,64,128]{3,2,1,0:T(8,128)(2,1)S(1)}, u32[]{:S(2)}, u32[]{:S(2)}) collective-permute-start(bf16[12,2,64,128]{3,2,1,0:T(8,128)(2,1)S(1)} %fusion.3), channel_id=1, source_target_pairs={{0,8},{8,0},{1,9},{9,1},{2,10},{10,2},{3,11},{11,3},{4,12},{12,4},... | collective-permute-start | bytes 1179656 | tf_op jit(solution)/shard_map/ppermute | solution.py:28
  69.9 17.9 %collective-permute-start.2 = (bf16[12,2,128,128]{3,2,1,0:T(8,128)(2,1)S(1)}, bf16[12,2,128,128]{3,2,1,0:T(8,128)(2,1)S(1)}, u32[]{:S(2)}, u32[]{:S(2)}) collective-permute-start(bf16[12,2,128,128]{3,2,1,0:T(8,128)(2,1)S(1)} %slice_select_fusion), channel_id=1, source_target_pairs={{0,8},{8,0},{1,9},{9,1},{2,10},{10,2},{3,11},{11,3},{4,12},{12,4},... | collective-permute-start | bytes 2359304 | tf_op jit(solution)/shard_map/ppermute | solution.py:28
  89.7 11.3 %collective-permute-start.3 = (bf16[2,8,128,128]{3,2,1,0:T(8,128)(2,1)S(1)}, bf16[2,8,128,128]{3,2,1,0:T(8,128)(2,1)S(1)}, u32[]{:S(2)}, u32[]{:S(2)}) collective-permute-start(bf16[2,8,128,128]{3,2,1,0:T(8,128)(2,1)S(1)} %slice_select_fusion.1), channel_id=1, source_target_pairs={{0,16},{16,0},{1,17},{17,1},{2,18},{18,2},{3,19},{19,3},{4,20},{20... | collective-permute-start | bytes 1572872 | tf_op jit(solution)/shard_map/ppermute | solution.py:28
  90.9 10.7 %copy-start.4 = (bf16[192,64]{1,0:T(8,128)(2,1)S(1)}, bf16[192,64]{1,0:T(8,128)(2,1)}, u32[]{:S(2)}) copy-start(bf16[192,64]{1,0:T(8,128)(2,1)} %copy.12.w_t) | copy-start | bytes 73732
  90.9 10.7 %copy-start.5 = (f32[64,1]{1,0:T(8,128)S(1)}, f32[64,1]{1,0:T(8,128)}, u32[]{:S(2)}) copy-start(f32[64,1]{1,0:T(8,128)} %copy.11.gain) | copy-start | bytes 772
  91.0 10.6 %copy-start.1 = (bf16[8,8,64,128]{3,2,1,0:T(8,128)(2,1)S(1)}, bf16[8,8,64,128]{3,2,1,0:T(8,128)(2,1)}, u32[]{:S(2)}) copy-start(bf16[8,8,64,128]{3,2,1,0:T(8,128)(2,1)} %cot.3) | copy-start | bytes 3145732
  91.0 10.6 %copy-start.2 = (bf16[8,8,64,128]{3,2,1,0:T(8,128)(2,1)S(1)}, bf16[8,8,64,128]{3,2,1,0:T(8,128)(2,1)}, u32[]{:S(2)}) copy-start(bf16[8,8,64,128]{3,2,1,0:T(8,128)(2,1)} %get-tuple-element.58.dq) | copy-start | bytes 3145732
  91.0 10.6 %copy-start.3 = (bf16[8,8,64,128]{3,2,1,0:T(8,128)(2,1)S(1)}, bf16[8,8,64,128]{3,2,1,0:T(8,128)(2,1)}, u32[]{:S(2)}) copy-start(bf16[8,8,64,128]{3,2,1,0:T(8,128)(2,1)} %get-tuple-element.60.att) | copy-start | bytes 3145732
  108.4 1.3 collective-permute-start.4
  109.7 4.4 %collective-permute-start.5 = (f32[72,256]{1,0:T(8,128)S(1)}, f32[72,256]{1,0:T(8,128)S(1)}, u32[]{:S(2)}, u32[]{:S(2)}) collective-permute-start(f32[72,256]{1,0:T(8,128)S(1)} %add.47), channel_id=1, source_target_pairs={{0,2},{1,3},{2,0},{3,1},{4,6},{5,7},{6,4},{7,5},{8,10},{9,11},{10,... | collective-permute-start | bytes 221192 | tf_op jit(solution)/shard_map/ppermute | solution.py:266
  114.1 6.1 %collective-permute-start.6 = (f32[72,256]{1,0:T(8,128)S(1)}, f32[72,256]{1,0:T(8,128)S(1)}, u32[]{:S(2)}, u32[]{:S(2)}) collective-permute-start(f32[72,256]{1,0:T(8,128)S(1)} %add.48), channel_id=1, source_target_pairs={{0,4},{1,5},{2,6},{3,7},{4,0},{5,1},{6,2},{7,3},{8,12},{9,13},{10,... | collective-permute-start | bytes 221192 | tf_op jit(solution)/shard_map/ppermute | solution.py:266
  120.2 4.4 %collective-permute-start.7 = (f32[72,256]{1,0:T(8,128)S(1)}, f32[72,256]{1,0:T(8,128)S(1)}, u32[]{:S(2)}, u32[]{:S(2)}) collective-permute-start(f32[72,256]{1,0:T(8,128)S(1)} %add.49), channel_id=1, source_target_pairs={{0,8},{8,0},{1,9},{9,1},{2,10},{10,2},{3,11},{11,3},{4,12},{12,4},... | collective-permute-start | bytes 221192 | tf_op jit(solution)/shard_map/ppermute | solution.py:266
  124.6 4.4 %collective-permute-start.8 = (f32[72,256]{1,0:T(8,128)S(1)}, f32[72,256]{1,0:T(8,128)S(1)}, u32[]{:S(2)}, u32[]{:S(2)}) collective-permute-start(f32[72,256]{1,0:T(8,128)S(1)} %add.50), channel_id=1, source_target_pairs={{0,16},{16,0},{1,17},{17,1},{2,18},{18,2},{3,19},{19,3},{4,20},{20... | collective-permute-start | bytes 221192 | tf_op jit(solution)/shard_map/ppermute | solution.py:266

commit v4 on v3

--- a/solution.py
+++ b/solution.py
@@ -287,13 +287,69 @@
     return own.at[first].add(from_before).at[last].add(from_after)
 
 
+def firsts():
+    return lax.axis_index("vrow") == 0, lax.axis_index("vcol") == 0
+
+
+def both_sides(first, block):
+    none = jnp.zeros_like(block)
+    return jnp.where(first, none, block), jnp.where(first, block, none)
+
+
+def swap_all(row_block, col_block, corner):
+    swap = [(0, 1), (1, 0)]
+    return (
+        lax.ppermute(col_block, "vcol", swap),
+        lax.ppermute(row_block, "vrow", swap),
+        lax.ppermute(corner, ("vrow", "vcol"), [(i, 3 - i) for i in range(4)]),
+    )
+
+
+def paired():
+    return lax.axis_size("vrow") == 2 and lax.axis_size("vcol") == 2
+
+
+def extend_views(block):
+    if not paired():
+        return extended(extended(block, "vrow", 0), "vcol", 1)
+    first_r, first_c = firsts()
+    row_send = jnp.where(first_r, block[-REACH:], block[:REACH])
+    col_send = jnp.where(first_c, block[:, -REACH:], block[:, :REACH])
+    corner = jnp.where(first_c, row_send[:, -REACH:], row_send[:, :REACH])
+    col, row, corner = swap_all(row_send, col_send, corner)
+    left, right = both_sides(first_c, col)
+    corner_left, corner_right = both_sides(first_c, corner)
+    strip = jnp.concatenate([corner_left, row, corner_right], axis=1)
+    above, below = both_sides(first_r, strip)
+    middle = jnp.concatenate([left, block, right], axis=1)
+    return jnp.concatenate([above, middle, below], axis=0)
+
+
+def fold_views(block):
+    if not paired():
+        return folded(folded(block, "vcol", 1), "vrow", 0)
+    first_r, first_c = firsts()
+    inner = slice(REACH, -REACH)
+    strip = jnp.where(first_r, block[-REACH:], block[:REACH])
+    col_send = jnp.where(first_c, block[inner, -REACH:], block[inner, :REACH])
+    corner = jnp.where(first_c, strip[:, -REACH:], strip[:, :REACH])
+    col, row, corner = swap_all(strip[:, inner], col_send, corner)
+    corner_left, corner_right = both_sides(first_c, corner)
+    row = row.at[:, :REACH].add(corner_left).at[:, -REACH:].add(corner_right)
+    left, right = both_sides(first_c, col)
+    above, below = both_sides(first_r, row)
+    own = block[inner, inner]
+    own = own.at[:, :REACH].add(left).at[:, -REACH:].add(right)
+    return own.at[:REACH].add(above).at[-REACH:].add(below)
+
+
 def body(features, out_cotangent, norm_gain, query_proj, keyval_proj, output_proj):
     gain = norm_gain[:, None]
     w_all = jnp.concatenate([query_proj, keyval_proj], axis=1)
     w_t = w_all.T
-    feat_pad = extended(extended(features, "vrow", 0), "vcol", 1)
+    feat_pad = extend_views(features)
     dq, att, dkv = attend(feat_pad, out_cotangent, gain, w_t, output_proj)
-    dkv = folded(folded(dkv, "vcol", 1), "vrow", 0)
+    dkv = fold_views(dkv)
     rows, cols, chans, pix = features.shape
     axes = ("vrow", "vcol", "pix")
     tokens_all = rows * cols * pix * math.prod(lax.axis_size(a) for a in axes)

time: 131 us -> 112 us (0.85)
  waiting for transfers between devices: 55.3 us -> 29.4 us
  starting transfers between devices: 10.4 us -> 14.7 us
  other arithmetic: 8.13 us -> 10 us
    ppermute x4 -> x6, waiting for transfers between devices: 37.6 us -> 15.9 us  [the longest x2 11.4 us: swap_all(): lax.ppermute(col_block, 'vcol', swap)]
    ppermute x5, waiting for transfers between devices: 17.6 us -> 13.5 us  [summed(): lax.ppermute(block, axis, [(i, i ^ hop) for i in range(count)])]
    ppermute x5, starting transfers between devices: 2.99 us -> 6.33 us  [summed(): lax.ppermute(block, axis, [(i, i ^ hop) for i in range(count)])]
    select_n x6 -> x9, other arithmetic: 3.88 us -> 5.07 us  [the longest x1 1.46 us: fold_views(): strip = jnp.where(first_r, block[-REACH:], block[:REACH])]
    ppermute x4 -> x6, starting transfers between devices: 7.43 us -> 8.36 us  [the longest x2 4.79 us: swap_all(): lax.ppermute(row_block, 'vrow', swap)]
  transfers between devices with their start and end apart: 9 -> 11, of which waited for: 9 -> 9; matrix products, arithmetic and copies ran while one was open for 3% -> 8% of each run, Pallas kernels for 0% -> 0%
where the time goes in v4:
time: 112 us; the launch traced here: 111 us
  Pallas kernels  50.7 us (45%)
  waiting for transfers between devices  29.4 us (26%)
  starting transfers between devices  14.7 us (13%)
  other arithmetic  10 us (9%)
  local copies, waits for them, and re-layouts  5.78 us (5%)
    pallas_call x1, Pallas kernels, attend(): pl.pallas_call(attend_kernel, out_shape=(jax.ShapeDtypeStruct(cot.shape,...  43.9 us
    ppermute x5, waiting for transfers between devices, summed(): lax.ppermute(block, axis, [(i, i ^ hop) for i in range(count)])  13.5 us
    ppermute x2, waiting for transfers between devices, swap_all(): lax.ppermute(col_block, 'vcol', swap)  11.4 us
    pallas_call x1, Pallas kernels, back(): pl.pallas_call(functools.partial(back_kernel, factor), grid=(rows,), out_...  6.78 us
    ppermute x5, starting transfers between devices, summed(): lax.ppermute(block, axis, [(i, i ^ hop) for i in range(count)])  6.33 us
    ppermute x2, starting transfers between devices, swap_all(): lax.ppermute(row_block, 'vrow', swap)  4.79 us
    ppermute x2, waiting for transfers between devices, swap_all(): lax.ppermute(row_block, 'vrow', swap)  3.68 us
    ppermute x2, starting transfers between devices, swap_all(): lax.ppermute(corner, ('vrow', 'vcol'), [(i, 3 - i) for i in range(4)])  2.3 us
  transfers between devices with their start and end apart: 11, of which 9 were waited for; matrix products, arithmetic and copies ran while one was open for 8% of the time, Pallas kernels for 0%

profile of v4, /device:TPU:0, one launch (start us, length us, event | category | flops | bytes accessed | tf_op | source)
XLA Modules:
  0.0 111.4 jit_solution(14627561533858620591)
XLA Ops:
  0.6 0.0 copy-start
  0.6 1.1 %slice_select_fusion.3 = bf16[2,8,64,128]{3,2,1,0:T(8,128)(2,1)S(1)} fusion(bf16[8,8,64,128]{3,2,1,0:T(8,128)(2,1)} %feat.1, pred[]{:T(512)S(6)} %eq.8), kind=kLoop, calls=%fused_computation.14 | loop fusion | flops 131072 | bytes 786433 | tf_op jit(solution)/shard_map/jit(_where)/select_n | solution.py:316
  1.8 3.0 %collective-permute-start.1 = (bf16[2,8,64,128]{3,2,1,0:T(8,128)(2,1)S(1)}, bf16[2,8,64,128]{3,2,1,0:T(8,128)(2,1)S(1)}, u32[]{:S(2)}, u32[]{:S(2)}) collective-permute-start(bf16[2,8,64,128]{3,2,1,0:T(8,128)(2,1)S(1)} %slice_select_fusion.3), channel_id=1, source_target_pairs={{0,16},{16,0},{1,17},{17,1},{2,18},{18,2},{3,19},{19,3},{4,20},{20... | collective-permute-start | bytes 786440 | tf_op jit(solution)/shard_map/ppermute | solution.py:303
  4.8 1.5 %collective-permute-start = (bf16[2,2,64,128]{3,2,1,0:T(8,128)(2,1)S(1)}, bf16[2,2,64,128]{3,2,1,0:T(8,128)(2,1)S(1)}, u32[]{:S(2)}, u32[]{:S(2)}) collective-permute-start(bf16[2,2,64,128]{3,2,1,0:T(8,128)(2,1)S(1)} %slice_select_fusion.5), channel_id=1, source_target_pairs={{0,24},{8,16},{16,8},{24,0},{1,25},{9,17},{17,9},{25,1},{2,26},{10... | collective-permute-start | bytes 196616 | tf_op jit(solution)/shard_map/ppermute | solution.py:304
  6.3 1.1 slice_select_fusion.2
  7.4 0.1 collective-permute-start.2
  7.6 0.8 pad_maximum_fusion.2
  8.4 1.4 %copy.11.gain = f32[64,1]{1,0:T(8,128)} copy(f32[64,1]{0,1:T(1,128)} %bitcast.5) | data formatting | bytes 512 | tf_op jit(solution)/shard_map/broadcast_in_dim | solution.py:347
  9.7 0.7 copy.12.w_t
  10.4 0.0 collective-permute-done
  10.5 4.5 %collective-permute-done.2 = bf16[8,2,64,128]{3,2,1,0:T(8,128)(2,1)S(1)} collective-permute-done((bf16[8,2,64,128]{3,2,1,0:T(8,128)(2,1)S(1)}, bf16[8,2,64,128]{3,2,1,0:T(8,128)(2,1)S(1)}, u32[]{:S(2)}, u32[]{:S(2)}) %collective-permute-start.2) | collective-permute-done | bytes 262176 | tf_op jit(solution)/shard_map/ppermute | solution.py:302
  15.0 0.0 collective-permute-done.1
  15.0 0.1 broadcast_select_fusion.1
  15.1 0.0 copy-done
  15.1 1.7 %pad_maximum_fusion.feat = bf16[12,12,64,128]{3,2,1,0:T(8,128)(2,1)} fusion(bf16[2,12,64,128]{3,2,1,0:T(8,128)(2,1)S(1)} %get-tuple-element.88, bf16[8,2,64,128]{3,2,1,0:T(8,128)(2,1)S(1)} %get-tuple-element.90, bf16[8,8,64,128]{3,2,1,0:T(8,128)(2,1)S(1)} %copy-done, bf16[8,2,64,128]{3,2,1,0:T(8,128)(2,1)S(1)} %get-tuple-element.89, ...), kind=kLoop, calls=%fused_computation | loop fusion | flops 4718592 | bytes 4718592 | tf_op jit(solution)/shard_map/concatenate | solution.py:325
  16.8 43.9 %attend.1 = (bf16[8,8,64,128]{3,2,1,0:T(8,128)(2,1)}, bf16[8,8,64,128]{3,2,1,0:T(8,128)(2,1)}, bf16[12,12,128,128]{3,2,1,0:T(8,128)(2,1)}) custom-call(bf16[12,12,64,128]{3,2,1,0:T(8,128)(2,1)} %pad_maximum_fusion.feat, bf16[8,8,64,128]{3,2,1,0:T(8,128)(2,1)} %cot.3, f32[64,1]{1,0:T(8,128)} %copy.11.gain, bf16[192,64]{1,0:T(8,128)(2,1)} %copy.12.w_t, ...), custom_call_target="tpu_custom_call" | custom-call | tf_op jit(solution)/shard_map/attend/pallas_call | solution.py:175
  60.7 1.3 %slice_select_fusion.1 = bf16[8,2,128,128]{3,2,1,0:T(8,128)(2,1)S(1)} fusion(bf16[12,12,128,128]{3,2,1,0:T(8,128)(2,1)} %get-tuple-element.83, pred[]{:T(512)S(6)} %eq.9), kind=kLoop, calls=%fused_computation.9 | loop fusion | flops 262144 | bytes 1572865 | tf_op jit(solution)/shard_map/jit(_where)/select_n | solution.py:334
  62.0 1.1 %collective-permute-start.3 = (bf16[8,2,128,128]{3,2,1,0:T(8,128)(2,1)S(1)}, bf16[8,2,128,128]{3,2,1,0:T(8,128)(2,1)S(1)}, u32[]{:S(2)}, u32[]{:S(2)}) collective-permute-start(bf16[8,2,128,128]{3,2,1,0:T(8,128)(2,1)S(1)} %slice_select_fusion.1), channel_id=1, source_target_pairs={{0,8},{8,0},{1,9},{9,1},{2,10},{10,2},{3,11},{11,3},{4,12},{12,4},... | collective-permute-start | bytes 1572872 | tf_op jit(solution)/shard_map/ppermute | solution.py:302
  63.1 1.7 %slice.235 = bf16[8,8,128,128]{3,2,1,0:T(8,128)(2,1)S(1)} slice(bf16[12,12,128,128]{3,2,1,0:T(8,128)(2,1)} %get-tuple-element.83), slice={[2:10], [2:10], [0:128], [0:128]} | slice | bytes 4194304 | tf_op jit(solution)/shard_map/slice | solution.py:341
  64.8 1.5 %slice_select_fusion = bf16[2,12,128,128]{3,2,1,0:T(8,128)(2,1)S(1)} fusion(bf16[12,12,128,128]{3,2,1,0:T(8,128)(2,1)} %get-tuple-element.83, pred[]{:T(512)S(6)} %eq.8), kind=kLoop, calls=%fused_computation.1 | loop fusion | flops 393216 | bytes 2359297 | tf_op jit(solution)/shard_map/jit(_where)/select_n | solution.py:333
  66.4 1.8 %collective-permute-start.4 = (bf16[2,8,128,128]{3,2,1,0:T(8,128)(2,1)S(1)}, bf16[2,8,128,128]{3,2,1,0:T(8,128)(2,1)S(1)}, u32[]{:S(2)}, u32[]{:S(2)}) collective-permute-start(bf16[2,8,128,128]{3,2,1,0:T(8,128)(2,1)S(1)} %slice.257), channel_id=1, source_target_pairs={{0,16},{16,0},{1,17},{17,1},{2,18},{18,2},{3,19},{19,3},{4,20},{20... | collective-permute-start | bytes 1572872 | tf_op jit(solution)/shard_map/ppermute | solution.py:303
  68.1 0.8 collective-permute-start.5
  68.9 6.9 %collective-permute-done.3 = bf16[8,2,128,128]{3,2,1,0:T(8,128)(2,1)S(1)} collective-permute-done((bf16[8,2,128,128]{3,2,1,0:T(8,128)(2,1)S(1)}, bf16[8,2,128,128]{3,2,1,0:T(8,128)(2,1)S(1)}, u32[]{:S(2)}, u32[]{:S(2)}) %collective-permute-start.3) | collective-permute-done | bytes 524320 | tf_op jit(solution)/shard_map/ppermute | solution.py:302
  75.8 1.2 %add_dynamic-update-slice_fusion = bf16[8,8,128,128]{3,2,1,0:T(8,128)(2,1)S(1)} fusion(bf16[8,8,128,128]{3,2,1,0:T(8,128)(2,1)S(1)} %slice.235, bf16[8,2,128,128]{3,2,1,0:T(8,128)(2,1)S(1)} %collective-permute-done.3, bf16[12,12,128,128]{3,2,1,0:T(8,128)(2,1)} %get-tuple-element.83, pred[]{:T(512)S(6)} %eq.9), kind=kLoop, calls=%fused_computation.8 | loop fusion | flops 1310720 | bytes 1572865 | tf_op jit(solution)/shard_map/scatter-add | solution.py:342
  77.1 0.3 fusion.2
  77.4 0.0 copy-start.1
  77.4 0.0 copy-start.2
  77.4 0.0 copy-start.3
  77.4 0.0 copy-start.4
  77.4 0.0 copy-start.5
  77.4 0.9 collective-permute-done.5
  78.3 3.7 %collective-permute-done.4 = bf16[2,8,128,128]{3,2,1,0:T(8,128)(2,1)S(1)} collective-permute-done((bf16[2,8,128,128]{3,2,1,0:T(8,128)(2,1)S(1)}, bf16[2,8,128,128]{3,2,1,0:T(8,128)(2,1)S(1)}, u32[]{:S(2)}, u32[]{:S(2)}) %collective-permute-start.4) | collective-permute-done | bytes 524320 | tf_op jit(solution)/shard_map/ppermute | solution.py:303
  82.0 0.1 fusion.4
  82.1 0.1 fusion.3
  82.2 0.3 fusion.1
  82.5 0.3 fusion.dkv
  82.8 0.0 copy-done.1
  82.8 0.0 copy-done.2
  82.8 0.0 copy-done.3
  82.8 0.0 copy-done.4
  82.8 0.0 copy-done.5
  82.8 6.8 %back.1 = (bf16[8,8,64,128]{3,2,1,0:T(8,128)(2,1)}, f32[72,256]{1,0:T(8,128)S(1)}) custom-call(bf16[8,8,64,128]{3,2,1,0:T(8,128)(2,1)S(1)} %copy-done, bf16[8,8,64,128]{3,2,1,0:T(8,128)(2,1)S(1)} %copy-done.1, bf16[8,8,64,128]{3,2,1,0:T(8,128)(2,1)S(1)} %copy-done.2, bf16[8,8,128,128]{3,2,1,0:T(8,128)(2,1)S(1)} %fusion.dkv, ...), custom_call_target="tpu_custom_call" | custom-call | tf_op jit(solution)/shard_map/back/pallas_call | solution.py:246
  89.6 0.0 collective-permute-start.6
  89.6 1.3 %collective-permute-done.6 = f32[72,256]{1,0:T(8,128)S(1)} collective-permute-done((f32[72,256]{1,0:T(8,128)S(1)}, f32[72,256]{1,0:T(8,128)S(1)}, u32[]{:S(2)}, u32[]{:S(2)}) %collective-permute-start.6) | collective-permute-done | bytes 73760 | tf_op jit(solution)/shard_map/ppermute | solution.py:266
  90.9 1.7 %collective-permute-start.7 = (f32[72,256]{1,0:T(8,128)S(1)}, f32[72,256]{1,0:T(8,128)S(1)}, u32[]{:S(2)}, u32[]{:S(2)}) collective-permute-start(f32[72,256]{1,0:T(8,128)S(1)} %add.63), channel_id=1, source_target_pairs={{0,2},{1,3},{2,0},{3,1},{4,6},{5,7},{6,4},{7,5},{8,10},{9,11},{10,... | collective-permute-start | bytes 221192 | tf_op jit(solution)/shard_map/ppermute | solution.py:266
  92.6 2.8 %collective-permute-done.7 = f32[72,256]{1,0:T(8,128)S(1)} collective-permute-done((f32[72,256]{1,0:T(8,128)S(1)}, f32[72,256]{1,0:T(8,128)S(1)}, u32[]{:S(2)}, u32[]{:S(2)}) %collective-permute-start.7) | collective-permute-done | bytes 73760 | tf_op jit(solution)/shard_map/ppermute | solution.py:266
  95.3 2.7 %collective-permute-start.8 = (f32[72,256]{1,0:T(8,128)S(1)}, f32[72,256]{1,0:T(8,128)S(1)}, u32[]{:S(2)}, u32[]{:S(2)}) collective-permute-start(f32[72,256]{1,0:T(8,128)S(1)} %add.64), channel_id=1, source_target_pairs={{0,4},{1,5},{2,6},{3,7},{4,0},{5,1},{6,2},{7,3},{8,12},{9,13},{10,... | collective-permute-start | bytes 221192 | tf_op jit(solution)/shard_map/ppermute | solution.py:266
  98.0 2.6 %collective-permute-done.8 = f32[72,256]{1,0:T(8,128)S(1)} collective-permute-done((f32[72,256]{1,0:T(8,128)S(1)}, f32[72,256]{1,0:T(8,128)S(1)}, u32[]{:S(2)}, u32[]{:S(2)}) %collective-permute-start.8) | collective-permute-done | bytes 73760 | tf_op jit(solution)/shard_map/ppermute | solution.py:266
  100.7 0.4 collective-permute-start.9
  101.0 4.1 %collective-permute-done.9 = f32[72,256]{1,0:T(8,128)S(1)} collective-permute-done((f32[72,256]{1,0:T(8,128)S(1)}, f32[72,256]{1,0:T(8,128)S(1)}, u32[]{:S(2)}, u32[]{:S(2)}) %collective-permute-start.9) | collective-permute-done | bytes 73760 | tf_op jit(solution)/shard_map/ppermute | solution.py:266
  105.1 1.6 %collective-permute-start.10 = (f32[72,256]{1,0:T(8,128)S(1)}, f32[72,256]{1,0:T(8,128)S(1)}, u32[]{:S(2)}, u32[]{:S(2)}) collective-permute-start(f32[72,256]{1,0:T(8,128)S(1)} %add.66), channel_id=1, source_target_pairs={{0,16},{16,0},{1,17},{17,1},{2,18},{18,2},{3,19},{19,3},{4,20},{20... | collective-permute-start | bytes 221192 | tf_op jit(solution)/shard_map/ppermute | solution.py:266
  106.7 2.8 %collective-permute-done.10 = f32[72,256]{1,0:T(8,128)S(1)} collective-permute-done((f32[72,256]{1,0:T(8,128)S(1)}, f32[72,256]{1,0:T(8,128)S(1)}, u32[]{:S(2)}, u32[]{:S(2)}) %collective-permute-start.10) | collective-permute-done | bytes 73760 | tf_op jit(solution)/shard_map/ppermute | solution.py:266
  109.5 0.7 fusion.6
  110.2 0.7 slice.264
  110.9 0.5 slice_bitcast_fusion
  (10 shorter events, 0.2 us)
Async XLA Ops:
  0.6 14.5 %copy-start = (bf16[8,8,64,128]{3,2,1,0:T(8,128)(2,1)S(1)}, bf16[8,8,64,128]{3,2,1,0:T(8,128)(2,1)}, u32[]{:S(2)}) copy-start(bf16[8,8,64,128]{3,2,1,0:T(8,128)(2,1)} %feat.1) | copy-start | bytes 3145732
  1.8 13.2 %collective-permute-start.1 = (bf16[2,8,64,128]{3,2,1,0:T(8,128)(2,1)S(1)}, bf16[2,8,64,128]{3,2,1,0:T(8,128)(2,1)S(1)}, u32[]{:S(2)}, u32[]{:S(2)}) collective-permute-start(bf16[2,8,64,128]{3,2,1,0:T(8,128)(2,1)S(1)} %slice_select_fusion.3), channel_id=1, source_target_pairs={{0,16},{16,0},{1,17},{17,1},{2,18},{18,2},{3,19},{19,3},{4,20},{20... | collective-permute-start | bytes 786440 | tf_op jit(solution)/shard_map/ppermute | solution.py:303
  4.8 5.6 %collective-permute-start = (bf16[2,2,64,128]{3,2,1,0:T(8,128)(2,1)S(1)}, bf16[2,2,64,128]{3,2,1,0:T(8,128)(2,1)S(1)}, u32[]{:S(2)}, u32[]{:S(2)}) collective-permute-start(bf16[2,2,64,128]{3,2,1,0:T(8,128)(2,1)S(1)} %slice_select_fusion.5), channel_id=1, source_target_pairs={{0,24},{8,16},{16,8},{24,0},{1,25},{9,17},{17,9},{25,1},{2,26},{10... | collective-permute-start | bytes 196616 | tf_op jit(solution)/shard_map/ppermute | solution.py:304
  7.4 7.6 %collective-permute-start.2 = (bf16[8,2,64,128]{3,2,1,0:T(8,128)(2,1)S(1)}, bf16[8,2,64,128]{3,2,1,0:T(8,128)(2,1)S(1)}, u32[]{:S(2)}, u32[]{:S(2)}) collective-permute-start(bf16[8,2,64,128]{3,2,1,0:T(8,128)(2,1)S(1)} %slice_select_fusion.2), channel_id=1, source_target_pairs={{0,8},{8,0},{1,9},{9,1},{2,10},{10,2},{3,11},{11,3},{4,12},{12,4},... | collective-permute-start | bytes 786440 | tf_op jit(solution)/shard_map/ppermute | solution.py:302
  62.0 13.8 %collective-permute-start.3 = (bf16[8,2,128,128]{3,2,1,0:T(8,128)(2,1)S(1)}, bf16[8,2,128,128]{3,2,1,0:T(8,128)(2,1)S(1)}, u32[]{:S(2)}, u32[]{:S(2)}) collective-permute-start(bf16[8,2,128,128]{3,2,1,0:T(8,128)(2,1)S(1)} %slice_select_fusion.1), channel_id=1, source_target_pairs={{0,8},{8,0},{1,9},{9,1},{2,10},{10,2},{3,11},{11,3},{4,12},{12,4},... | collective-permute-start | bytes 1572872 | tf_op jit(solution)/shard_map/ppermute | solution.py:302
  66.4 15.6 %collective-permute-start.4 = (bf16[2,8,128,128]{3,2,1,0:T(8,128)(2,1)S(1)}, bf16[2,8,128,128]{3,2,1,0:T(8,128)(2,1)S(1)}, u32[]{:S(2)}, u32[]{:S(2)}) collective-permute-start(bf16[2,8,128,128]{3,2,1,0:T(8,128)(2,1)S(1)} %slice.257), channel_id=1, source_target_pairs={{0,16},{16,0},{1,17},{17,1},{2,18},{18,2},{3,19},{19,3},{4,20},{20... | collective-permute-start | bytes 1572872 | tf_op jit(solution)/shard_map/ppermute | solution.py:303
  68.1 10.2 %collective-permute-start.5 = (bf16[2,2,128,128]{3,2,1,0:T(8,128)(2,1)S(1)}, bf16[2,2,128,128]{3,2,1,0:T(8,128)(2,1)S(1)}, u32[]{:S(2)}, u32[]{:S(2)}) collective-permute-start(bf16[2,2,128,128]{3,2,1,0:T(8,128)(2,1)S(1)} %slice_select_fusion.4), channel_id=1, source_target_pairs={{0,24},{8,16},{16,8},{24,0},{1,25},{9,17},{17,9},{25,1},{2,26},{10... | collective-permute-start | bytes 393224 | tf_op jit(solution)/shard_map/ppermute | solution.py:304
  77.4 5.4 %copy-start.1 = (bf16[8,8,64,128]{3,2,1,0:T(8,128)(2,1)S(1)}, bf16[8,8,64,128]{3,2,1,0:T(8,128)(2,1)}, u32[]{:S(2)}) copy-start(bf16[8,8,64,128]{3,2,1,0:T(8,128)(2,1)} %cot.3) | copy-start | bytes 3145732
  77.4 5.4 %copy-start.2 = (bf16[8,8,64,128]{3,2,1,0:T(8,128)(2,1)S(1)}, bf16[8,8,64,128]{3,2,1,0:T(8,128)(2,1)}, u32[]{:S(2)}) copy-start(bf16[8,8,64,128]{3,2,1,0:T(8,128)(2,1)} %get-tuple-element.82.dq) | copy-start | bytes 3145732
  77.4 5.4 %copy-start.3 = (bf16[8,8,64,128]{3,2,1,0:T(8,128)(2,1)S(1)}, bf16[8,8,64,128]{3,2,1,0:T(8,128)(2,1)}, u32[]{:S(2)}) copy-start(bf16[8,8,64,128]{3,2,1,0:T(8,128)(2,1)} %get-tuple-element.84.att) | copy-start | bytes 3145732
  77.4 5.4 %copy-start.4 = (bf16[192,64]{1,0:T(8,128)(2,1)S(1)}, bf16[192,64]{1,0:T(8,128)(2,1)}, u32[]{:S(2)}) copy-start(bf16[192,64]{1,0:T(8,128)(2,1)} %copy.12.w_t) | copy-start | bytes 73732
  77.4 5.4 %copy-start.5 = (f32[64,1]{1,0:T(8,128)S(1)}, f32[64,1]{1,0:T(8,128)}, u32[]{:S(2)}) copy-start(f32[64,1]{1,0:T(8,128)} %copy.11.gain) | copy-start | bytes 772
  89.6 1.3 %collective-permute-start.6 = (f32[72,256]{1,0:T(8,128)S(1)}, f32[72,256]{1,0:T(8,128)S(1)}, u32[]{:S(2)}, u32[]{:S(2)}) collective-permute-start(f32[72,256]{1,0:T(8,128)S(1)} %get-tuple-element.86), channel_id=1, source_target_pairs={{0,1},{1,0},{2,3},{3,2},{4,5},{5,4},{6,7},{7,6},{8,9},{9,8},{10,11... | collective-permute-start | bytes 221192 | tf_op jit(solution)/shard_map/ppermute | solution.py:266
  90.9 4.4 %collective-permute-start.7 = (f32[72,256]{1,0:T(8,128)S(1)}, f32[72,256]{1,0:T(8,128)S(1)}, u32[]{:S(2)}, u32[]{:S(2)}) collective-permute-start(f32[72,256]{1,0:T(8,128)S(1)} %add.63), channel_id=1, source_target_pairs={{0,2},{1,3},{2,0},{3,1},{4,6},{5,7},{6,4},{7,5},{8,10},{9,11},{10,... | collective-permute-start | bytes 221192 | tf_op jit(solution)/shard_map/ppermute | solution.py:266
  95.3 5.3 %collective-permute-start.8 = (f32[72,256]{1,0:T(8,128)S(1)}, f32[72,256]{1,0:T(8,128)S(1)}, u32[]{:S(2)}, u32[]{:S(2)}) collective-permute-start(f32[72,256]{1,0:T(8,128)S(1)} %add.64), channel_id=1, source_target_pairs={{0,4},{1,5},{2,6},{3,7},{4,0},{5,1},{6,2},{7,3},{8,12},{9,13},{10,... | collective-permute-start | bytes 221192 | tf_op jit(solution)/shard_map/ppermute | solution.py:266
  100.7 4.4 %collective-permute-start.9 = (f32[72,256]{1,0:T(8,128)S(1)}, f32[72,256]{1,0:T(8,128)S(1)}, u32[]{:S(2)}, u32[]{:S(2)}) collective-permute-start(f32[72,256]{1,0:T(8,128)S(1)} %add.65), channel_id=1, source_target_pairs={{0,8},{8,0},{1,9},{9,1},{2,10},{10,2},{3,11},{11,3},{4,12},{12,4},... | collective-permute-start | bytes 221192 | tf_op jit(solution)/shard_map/ppermute | solution.py:266
  105.1 4.4 %collective-permute-start.10 = (f32[72,256]{1,0:T(8,128)S(1)}, f32[72,256]{1,0:T(8,128)S(1)}, u32[]{:S(2)}, u32[]{:S(2)}) collective-permute-start(f32[72,256]{1,0:T(8,128)S(1)} %add.66), channel_id=1, source_target_pairs={{0,16},{16,0},{1,17},{17,1},{2,18},{18,2},{3,19},{19,3},{4,20},{20... | collective-permute-start | bytes 221192 | tf_op jit(solution)/shard_map/ppermute | solution.py:266

commit v5 on v4

--- a/solution.py
+++ b/solution.py
@@ -256,15 +256,21 @@
 
 
 def summed(block, axes):
-    for axis in axes:
-        count = lax.axis_size(axis)
-        if count & (count - 1):
-            block = lax.psum(block, axis)
-            continue
-        hop = 1
-        while hop < count:
-            block = block + lax.ppermute(block, axis, [(i, i ^ hop) for i in range(count)])
-            hop *= 2
+    count = math.prod(lax.axis_size(a) for a in axes)
+    if count & (count - 1):
+        return lax.psum(block, axes)
+
+    def across(hop):
+        return lax.ppermute(block, axes, [(i, i ^ hop) for i in range(count)])
+
+    hop = 1
+    while hop < count:
+        if 4 * hop <= count:
+            near, far, corner = across(hop), across(2 * hop), across(3 * hop)
+            block = (block + near) + (far + corner)
+        else:
+            block = block + across(hop)
+        hop *= 4
     return block
 
 
@@ -356,7 +362,7 @@
     grad, sums = back(
         tokens_all**-0.5, features, out_cotangent, dq, dkv, att, gain, w_t, w_all
     )
-    sums = summed(sums, axes[::-1])
+    sums = summed(sums, axes)
     return (
         grad,
         sums[:chans, :chans],

time: 112 us -> 113 us (level)
  starting transfers between devices: 14.7 us -> 16.6 us
    ppermute x5 -> x7, starting transfers between devices: 6.33 us -> 8.21 us  [across(): return lax.ppermute(block, axes, [(i, i ^ hop) for i in range(count)])]
    ppermute x5 -> x7, waiting for transfers between devices: 13.5 us -> 13.1 us  [across(): return lax.ppermute(block, axes, [(i, i ^ hop) for i in range(count)])]
  transfers between devices with their start and end apart: 11 -> 13, of which waited for: 9 -> 9; matrix products, arithmetic and copies ran while one was open for 8% -> 8% of each run, Pallas kernels for 0% -> 0%
where the time goes in v5:
time: 113 us
  Pallas kernels  50.7 us (45%)
  waiting for transfers between devices  29 us (26%)
  starting transfers between devices  16.6 us (15%)
  other arithmetic  10 us (9%)
  local copies, waits for them, and re-layouts  5.78 us (5%)
    pallas_call x1, Pallas kernels, attend(): pl.pallas_call(attend_kernel, out_shape=(jax.ShapeDtypeStruct(cot.shape,...  43.9 us
    ppermute x7, waiting for transfers between devices, across(): return lax.ppermute(block, axes, [(i, i ^ hop) for i in range(count)])  13.1 us
    ppermute x2, waiting for transfers between devices, swap_all(): lax.ppermute(col_block, 'vcol', swap)  11.4 us
    ppermute x7, starting transfers between devices, across(): return lax.ppermute(block, axes, [(i, i ^ hop) for i in range(count)])  8.21 us
    pallas_call x1, Pallas kernels, back(): pl.pallas_call(functools.partial(back_kernel, factor), grid=(rows,), out_...  6.78 us
    ppermute x2, starting transfers between devices, swap_all(): lax.ppermute(row_block, 'vrow', swap)  4.8 us
    ppermute x2, waiting for transfers between devices, swap_all(): lax.ppermute(row_block, 'vrow', swap)  3.67 us
    ppermute x2, starting transfers between devices, swap_all(): lax.ppermute(corner, ('vrow', 'vcol'), [(i, 3 - i) for i in range(4)])  2.3 us
  transfers between devices with their start and end apart: 13, of which 9 were waited for; matrix products, arithmetic and copies ran while one was open for 8% of the time, Pallas kernels for 0%

profile of v5, /device:TPU:0, one launch (start us, length us, event | category | flops | bytes accessed | tf_op | source)
XLA Modules:
  0.0 112.9 jit_solution(4224280397460963371)
XLA Ops:
  0.6 0.0 copy-start
  0.6 1.1 %slice_select_fusion.3 = bf16[2,8,64,128]{3,2,1,0:T(8,128)(2,1)S(1)} fusion(bf16[8,8,64,128]{3,2,1,0:T(8,128)(2,1)} %feat.1, pred[]{:T(512)S(6)} %eq.8), kind=kLoop, calls=%fused_computation.14 | loop fusion | flops 131072 | bytes 786433 | tf_op jit(solution)/shard_map/jit(_where)/select_n | solution.py:322
  1.8 3.0 %collective-permute-start.1 = (bf16[2,8,64,128]{3,2,1,0:T(8,128)(2,1)S(1)}, bf16[2,8,64,128]{3,2,1,0:T(8,128)(2,1)S(1)}, u32[]{:S(2)}, u32[]{:S(2)}) collective-permute-start(bf16[2,8,64,128]{3,2,1,0:T(8,128)(2,1)S(1)} %slice_select_fusion.3), channel_id=1, source_target_pairs={{0,16},{16,0},{1,17},{17,1},{2,18},{18,2},{3,19},{19,3},{4,20},{20... | collective-permute-start | bytes 786440 | tf_op jit(solution)/shard_map/ppermute | solution.py:309
  4.8 1.5 %collective-permute-start = (bf16[2,2,64,128]{3,2,1,0:T(8,128)(2,1)S(1)}, bf16[2,2,64,128]{3,2,1,0:T(8,128)(2,1)S(1)}, u32[]{:S(2)}, u32[]{:S(2)}) collective-permute-start(bf16[2,2,64,128]{3,2,1,0:T(8,128)(2,1)S(1)} %slice_select_fusion.5), channel_id=1, source_target_pairs={{0,24},{8,16},{16,8},{24,0},{1,25},{9,17},{17,9},{25,1},{2,26},{10... | collective-permute-start | bytes 196616 | tf_op jit(solution)/shard_map/ppermute | solution.py:310
  6.3 1.1 slice_select_fusion.2
  7.4 0.1 collective-permute-start.2
  7.6 0.8 pad_maximum_fusion.2
  8.4 1.4 %copy.11.gain = f32[64,1]{1,0:T(8,128)} copy(f32[64,1]{0,1:T(1,128)} %bitcast.5) | data formatting | bytes 512 | tf_op jit(solution)/shard_map/broadcast_in_dim | solution.py:353
  9.7 0.7 copy.12.w_t
  10.4 0.0 collective-permute-done
  10.5 4.5 %collective-permute-done.2 = bf16[8,2,64,128]{3,2,1,0:T(8,128)(2,1)S(1)} collective-permute-done((bf16[8,2,64,128]{3,2,1,0:T(8,128)(2,1)S(1)}, bf16[8,2,64,128]{3,2,1,0:T(8,128)(2,1)S(1)}, u32[]{:S(2)}, u32[]{:S(2)}) %collective-permute-start.2) | collective-permute-done | bytes 262176 | tf_op jit(solution)/shard_map/ppermute | solution.py:308
  15.0 0.0 collective-permute-done.1
  15.0 0.1 broadcast_select_fusion.1
  15.1 0.0 copy-done
  15.1 1.7 %pad_maximum_fusion.feat = bf16[12,12,64,128]{3,2,1,0:T(8,128)(2,1)} fusion(bf16[2,12,64,128]{3,2,1,0:T(8,128)(2,1)S(1)} %get-tuple-element.88, bf16[8,2,64,128]{3,2,1,0:T(8,128)(2,1)S(1)} %get-tuple-element.90, bf16[8,8,64,128]{3,2,1,0:T(8,128)(2,1)S(1)} %copy-done, bf16[8,2,64,128]{3,2,1,0:T(8,128)(2,1)S(1)} %get-tuple-element.89, ...), kind=kLoop, calls=%fused_computation | loop fusion | flops 4718592 | bytes 4718592 | tf_op jit(solution)/shard_map/concatenate | solution.py:331
  16.8 43.9 %attend.1 = (bf16[8,8,64,128]{3,2,1,0:T(8,128)(2,1)}, bf16[8,8,64,128]{3,2,1,0:T(8,128)(2,1)}, bf16[12,12,128,128]{3,2,1,0:T(8,128)(2,1)}) custom-call(bf16[12,12,64,128]{3,2,1,0:T(8,128)(2,1)} %pad_maximum_fusion.feat, bf16[8,8,64,128]{3,2,1,0:T(8,128)(2,1)} %cot.3, f32[64,1]{1,0:T(8,128)} %copy.11.gain, bf16[192,64]{1,0:T(8,128)(2,1)} %copy.12.w_t, ...), custom_call_target="tpu_custom_call" | custom-call | tf_op jit(solution)/shard_map/attend/pallas_call | solution.py:175
  60.7 1.3 %slice_select_fusion.1 = bf16[8,2,128,128]{3,2,1,0:T(8,128)(2,1)S(1)} fusion(bf16[12,12,128,128]{3,2,1,0:T(8,128)(2,1)} %get-tuple-element.83, pred[]{:T(512)S(6)} %eq.9), kind=kLoop, calls=%fused_computation.9 | loop fusion | flops 262144 | bytes 1572865 | tf_op jit(solution)/shard_map/jit(_where)/select_n | solution.py:340
  62.0 1.1 collective-permute-start.3
  63.1 1.7 %slice.235 = bf16[8,8,128,128]{3,2,1,0:T(8,128)(2,1)S(1)} slice(bf16[12,12,128,128]{3,2,1,0:T(8,128)(2,1)} %get-tuple-element.83), slice={[2:10], [2:10], [0:128], [0:128]} | slice | bytes 4194304 | tf_op jit(solution)/shard_map/slice | solution.py:347
  64.8 1.5 %slice_select_fusion = bf16[2,12,128,128]{3,2,1,0:T(8,128)(2,1)S(1)} fusion(bf16[12,12,128,128]{3,2,1,0:T(8,128)(2,1)} %get-tuple-element.83, pred[]{:T(512)S(6)} %eq.8), kind=kLoop, calls=%fused_computation.1 | loop fusion | flops 393216 | bytes 2359297 | tf_op jit(solution)/shard_map/jit(_where)/select_n | solution.py:339
  66.4 1.8 %collective-permute-start.4 = (bf16[2,8,128,128]{3,2,1,0:T(8,128)(2,1)S(1)}, bf16[2,8,128,128]{3,2,1,0:T(8,128)(2,1)S(1)}, u32[]{:S(2)}, u32[]{:S(2)}) collective-permute-start(bf16[2,8,128,128]{3,2,1,0:T(8,128)(2,1)S(1)} %slice.257), channel_id=1, source_target_pairs={{0,16},{16,0},{1,17},{17,1},{2,18},{18,2},{3,19},{19,3},{4,20},{20... | collective-permute-start | bytes 1572872 | tf_op jit(solution)/shard_map/ppermute | solution.py:309
  68.1 0.8 collective-permute-start.5
  68.9 6.9 %collective-permute-done.3 = bf16[8,2,128,128]{3,2,1,0:T(8,128)(2,1)S(1)} collective-permute-done((bf16[8,2,128,128]{3,2,1,0:T(8,128)(2,1)S(1)}, bf16[8,2,128,128]{3,2,1,0:T(8,128)(2,1)S(1)}, u32[]{:S(2)}, u32[]{:S(2)}) %collective-permute-start.3) | collective-permute-done | bytes 524320 | tf_op jit(solution)/shard_map/ppermute | solution.py:308
  75.8 1.2 %add_dynamic-update-slice_fusion = bf16[8,8,128,128]{3,2,1,0:T(8,128)(2,1)S(1)} fusion(bf16[8,8,128,128]{3,2,1,0:T(8,128)(2,1)S(1)} %slice.235, bf16[8,2,128,128]{3,2,1,0:T(8,128)(2,1)S(1)} %collective-permute-done.3, bf16[12,12,128,128]{3,2,1,0:T(8,128)(2,1)} %get-tuple-element.83, pred[]{:T(512)S(6)} %eq.9), kind=kLoop, calls=%fused_computation.8 | loop fusion | flops 1310720 | bytes 1572865 | tf_op jit(solution)/shard_map/scatter-add | solution.py:348
  77.1 0.3 fusion.2
  77.4 0.0 copy-start.1
  77.4 0.0 copy-start.2
  77.4 0.0 copy-start.3
  77.4 0.0 copy-start.4
  77.4 0.0 copy-start.5
  77.4 0.9 collective-permute-done.5
  78.3 3.7 %collective-permute-done.4 = bf16[2,8,128,128]{3,2,1,0:T(8,128)(2,1)S(1)} collective-permute-done((bf16[2,8,128,128]{3,2,1,0:T(8,128)(2,1)S(1)}, bf16[2,8,128,128]{3,2,1,0:T(8,128)(2,1)S(1)}, u32[]{:S(2)}, u32[]{:S(2)}) %collective-permute-start.4) | collective-permute-done | bytes 524320 | tf_op jit(solution)/shard_map/ppermute | solution.py:309
  82.0 0.1 fusion.4
  82.1 0.1 fusion.3
  82.2 0.3 fusion.1
  82.5 0.3 fusion.dkv
  82.8 0.0 copy-done.1
  82.8 0.0 copy-done.2
  82.8 0.0 copy-done.3
  82.8 0.0 copy-done.4
  82.8 0.0 copy-done.5
  82.9 6.8 %back.1 = (bf16[8,8,64,128]{3,2,1,0:T(8,128)(2,1)}, f32[72,256]{1,0:T(8,128)S(1)}) custom-call(bf16[8,8,64,128]{3,2,1,0:T(8,128)(2,1)S(1)} %copy-done, bf16[8,8,64,128]{3,2,1,0:T(8,128)(2,1)S(1)} %copy-done.1, bf16[8,8,64,128]{3,2,1,0:T(8,128)(2,1)S(1)} %copy-done.2, bf16[8,8,128,128]{3,2,1,0:T(8,128)(2,1)S(1)} %fusion.dkv, ...), custom_call_target="tpu_custom_call" | custom-call | tf_op jit(solution)/shard_map/back/pallas_call | solution.py:246
  89.6 1.6 %collective-permute-start.7 = (f32[72,256]{1,0:T(8,128)S(1)}, f32[72,256]{1,0:T(8,128)S(1)}, u32[]{:S(2)}, u32[]{:S(2)}) collective-permute-start(f32[72,256]{1,0:T(8,128)S(1)} %get-tuple-element.86), channel_id=1, source_target_pairs={{0,2},{1,3},{2,0},{3,1},{4,6},{5,7},{6,4},{7,5},{8,10},{9,11},{10,... | collective-permute-start | bytes 221192 | tf_op jit(solution)/shard_map/ppermute | solution.py:264
  91.2 0.0 collective-permute-start.8
  91.2 0.5 collective-permute-start.6
  91.8 2.2 %collective-permute-done.7 = f32[72,256]{1,0:T(8,128)S(1)} collective-permute-done((f32[72,256]{1,0:T(8,128)S(1)}, f32[72,256]{1,0:T(8,128)S(1)}, u32[]{:S(2)}, u32[]{:S(2)}) %collective-permute-start.7) | collective-permute-done | bytes 73760 | tf_op jit(solution)/shard_map/ppermute | solution.py:264
  94.0 1.6 %collective-permute-done.8 = f32[72,256]{1,0:T(8,128)S(1)} collective-permute-done((f32[72,256]{1,0:T(8,128)S(1)}, f32[72,256]{1,0:T(8,128)S(1)}, u32[]{:S(2)}, u32[]{:S(2)}) %collective-permute-start.8) | collective-permute-done | bytes 73760 | tf_op jit(solution)/shard_map/ppermute | solution.py:264
  95.6 0.0 collective-permute-done.6
  95.6 0.4 collective-permute-start.10
  96.0 3.8 %collective-permute-start.11 = (f32[72,256]{1,0:T(8,128)S(1)}, f32[72,256]{1,0:T(8,128)S(1)}, u32[]{:S(2)}, u32[]{:S(2)}) collective-permute-start(f32[72,256]{1,0:T(8,128)S(1)} %add_add_fusion.1), channel_id=1, source_target_pairs={{0,12},{1,13},{2,14},{3,15},{4,8},{5,9},{6,10},{7,11},{8,4},{9,5},... | collective-permute-start | bytes 221192 | tf_op jit(solution)/shard_map/ppermute | solution.py:264
  99.7 0.3 collective-permute-start.9
  100.0 0.0 collective-permute-done.10
  100.0 5.6 %collective-permute-done.11 = f32[72,256]{1,0:T(8,128)S(1)} collective-permute-done((f32[72,256]{1,0:T(8,128)S(1)}, f32[72,256]{1,0:T(8,128)S(1)}, u32[]{:S(2)}, u32[]{:S(2)}) %collective-permute-start.11) | collective-permute-done | bytes 73760 | tf_op jit(solution)/shard_map/ppermute | solution.py:264
  105.7 0.9 collective-permute-done.9
  106.6 1.6 %collective-permute-start.12 = (f32[72,256]{1,0:T(8,128)S(1)}, f32[72,256]{1,0:T(8,128)S(1)}, u32[]{:S(2)}, u32[]{:S(2)}) collective-permute-start(f32[72,256]{1,0:T(8,128)S(1)} %add_add_fusion), channel_id=1, source_target_pairs={{0,16},{1,17},{2,18},{3,19},{4,20},{5,21},{6,22},{7,23},{8,24},{9,... | collective-permute-start | bytes 221192 | tf_op jit(solution)/shard_map/ppermute | solution.py:264
  108.2 2.8 %collective-permute-done.12 = f32[72,256]{1,0:T(8,128)S(1)} collective-permute-done((f32[72,256]{1,0:T(8,128)S(1)}, f32[72,256]{1,0:T(8,128)S(1)}, u32[]{:S(2)}, u32[]{:S(2)}) %collective-permute-start.12) | collective-permute-done | bytes 73760 | tf_op jit(solution)/shard_map/ppermute | solution.py:264
  111.0 0.7 fusion.6
  111.7 0.7 slice.264
  112.4 0.5 slice_bitcast_fusion
  (8 shorter events, 0.2 us)
Async XLA Ops:
  0.6 14.5 %copy-start = (bf16[8,8,64,128]{3,2,1,0:T(8,128)(2,1)S(1)}, bf16[8,8,64,128]{3,2,1,0:T(8,128)(2,1)}, u32[]{:S(2)}) copy-start(bf16[8,8,64,128]{3,2,1,0:T(8,128)(2,1)} %feat.1) | copy-start | bytes 3145732
  1.8 13.2 %collective-permute-start.1 = (bf16[2,8,64,128]{3,2,1,0:T(8,128)(2,1)S(1)}, bf16[2,8,64,128]{3,2,1,0:T(8,128)(2,1)S(1)}, u32[]{:S(2)}, u32[]{:S(2)}) collective-permute-start(bf16[2,8,64,128]{3,2,1,0:T(8,128)(2,1)S(1)} %slice_select_fusion.3), channel_id=1, source_target_pairs={{0,16},{16,0},{1,17},{17,1},{2,18},{18,2},{3,19},{19,3},{4,20},{20... | collective-permute-start | bytes 786440 | tf_op jit(solution)/shard_map/ppermute | solution.py:309
  4.8 5.6 %collective-permute-start = (bf16[2,2,64,128]{3,2,1,0:T(8,128)(2,1)S(1)}, bf16[2,2,64,128]{3,2,1,0:T(8,128)(2,1)S(1)}, u32[]{:S(2)}, u32[]{:S(2)}) collective-permute-start(bf16[2,2,64,128]{3,2,1,0:T(8,128)(2,1)S(1)} %slice_select_fusion.5), channel_id=1, source_target_pairs={{0,24},{8,16},{16,8},{24,0},{1,25},{9,17},{17,9},{25,1},{2,26},{10... | collective-permute-start | bytes 196616 | tf_op jit(solution)/shard_map/ppermute | solution.py:310
  7.4 7.6 %collective-permute-start.2 = (bf16[8,2,64,128]{3,2,1,0:T(8,128)(2,1)S(1)}, bf16[8,2,64,128]{3,2,1,0:T(8,128)(2,1)S(1)}, u32[]{:S(2)}, u32[]{:S(2)}) collective-permute-start(bf16[8,2,64,128]{3,2,1,0:T(8,128)(2,1)S(1)} %slice_select_fusion.2), channel_id=1, source_target_pairs={{0,8},{8,0},{1,9},{9,1},{2,10},{10,2},{3,11},{11,3},{4,12},{12,4},... | collective-permute-start | bytes 786440 | tf_op jit(solution)/shard_map/ppermute | solution.py:308
  62.0 13.8 %collective-permute-start.3 = (bf16[8,2,128,128]{3,2,1,0:T(8,128)(2,1)S(1)}, bf16[8,2,128,128]{3,2,1,0:T(8,128)(2,1)S(1)}, u32[]{:S(2)}, u32[]{:S(2)}) collective-permute-start(bf16[8,2,128,128]{3,2,1,0:T(8,128)(2,1)S(1)} %slice_select_fusion.1), channel_id=1, source_target_pairs={{0,8},{8,0},{1,9},{9,1},{2,10},{10,2},{3,11},{11,3},{4,12},{12,4},... | collective-permute-start | bytes 1572872 | tf_op jit(solution)/shard_map/ppermute | solution.py:308
  66.4 15.6 %collective-permute-start.4 = (bf16[2,8,128,128]{3,2,1,0:T(8,128)(2,1)S(1)}, bf16[2,8,128,128]{3,2,1,0:T(8,128)(2,1)S(1)}, u32[]{:S(2)}, u32[]{:S(2)}) collective-permute-start(bf16[2,8,128,128]{3,2,1,0:T(8,128)(2,1)S(1)} %slice.257), channel_id=1, source_target_pairs={{0,16},{16,0},{1,17},{17,1},{2,18},{18,2},{3,19},{19,3},{4,20},{20... | collective-permute-start | bytes 1572872 | tf_op jit(solution)/shard_map/ppermute | solution.py:309
  68.1 10.2 %collective-permute-start.5 = (bf16[2,2,128,128]{3,2,1,0:T(8,128)(2,1)S(1)}, bf16[2,2,128,128]{3,2,1,0:T(8,128)(2,1)S(1)}, u32[]{:S(2)}, u32[]{:S(2)}) collective-permute-start(bf16[2,2,128,128]{3,2,1,0:T(8,128)(2,1)S(1)} %slice_select_fusion.4), channel_id=1, source_target_pairs={{0,24},{8,16},{16,8},{24,0},{1,25},{9,17},{17,9},{25,1},{2,26},{10... | collective-permute-start | bytes 393224 | tf_op jit(solution)/shard_map/ppermute | solution.py:310
  77.4 5.4 %copy-start.1 = (bf16[8,8,64,128]{3,2,1,0:T(8,128)(2,1)S(1)}, bf16[8,8,64,128]{3,2,1,0:T(8,128)(2,1)}, u32[]{:S(2)}) copy-start(bf16[8,8,64,128]{3,2,1,0:T(8,128)(2,1)} %cot.3) | copy-start | bytes 3145732
  77.4 5.4 %copy-start.2 = (bf16[8,8,64,128]{3,2,1,0:T(8,128)(2,1)S(1)}, bf16[8,8,64,128]{3,2,1,0:T(8,128)(2,1)}, u32[]{:S(2)}) copy-start(bf16[8,8,64,128]{3,2,1,0:T(8,128)(2,1)} %get-tuple-element.82.dq) | copy-start | bytes 3145732
  77.4 5.4 %copy-start.3 = (bf16[8,8,64,128]{3,2,1,0:T(8,128)(2,1)S(1)}, bf16[8,8,64,128]{3,2,1,0:T(8,128)(2,1)}, u32[]{:S(2)}) copy-start(bf16[8,8,64,128]{3,2,1,0:T(8,128)(2,1)} %get-tuple-element.84.att) | copy-start | bytes 3145732
  77.4 5.4 %copy-start.4 = (bf16[192,64]{1,0:T(8,128)(2,1)S(1)}, bf16[192,64]{1,0:T(8,128)(2,1)}, u32[]{:S(2)}) copy-start(bf16[192,64]{1,0:T(8,128)(2,1)} %copy.12.w_t) | copy-start | bytes 73732
  77.4 5.4 %copy-start.5 = (f32[64,1]{1,0:T(8,128)S(1)}, f32[64,1]{1,0:T(8,128)}, u32[]{:S(2)}) copy-start(f32[64,1]{1,0:T(8,128)} %copy.11.gain) | copy-start | bytes 772
  89.6 4.4 %collective-permute-start.7 = (f32[72,256]{1,0:T(8,128)S(1)}, f32[72,256]{1,0:T(8,128)S(1)}, u32[]{:S(2)}, u32[]{:S(2)}) collective-permute-start(f32[72,256]{1,0:T(8,128)S(1)} %get-tuple-element.86), channel_id=1, source_target_pairs={{0,2},{1,3},{2,0},{3,1},{4,6},{5,7},{6,4},{7,5},{8,10},{9,11},{10,... | collective-permute-start | bytes 221192 | tf_op jit(solution)/shard_map/ppermute | solution.py:264
  91.2 4.3 %collective-permute-start.8 = (f32[72,256]{1,0:T(8,128)S(1)}, f32[72,256]{1,0:T(8,128)S(1)}, u32[]{:S(2)}, u32[]{:S(2)}) collective-permute-start(f32[72,256]{1,0:T(8,128)S(1)} %get-tuple-element.86), channel_id=1, source_target_pairs={{0,3},{1,2},{2,1},{3,0},{4,7},{5,6},{6,5},{7,4},{8,11},{9,10},{10,... | collective-permute-start | bytes 221192 | tf_op jit(solution)/shard_map/ppermute | solution.py:264
  91.2 4.3 %collective-permute-start.6 = (f32[72,256]{1,0:T(8,128)S(1)}, f32[72,256]{1,0:T(8,128)S(1)}, u32[]{:S(2)}, u32[]{:S(2)}) collective-permute-start(f32[72,256]{1,0:T(8,128)S(1)} %get-tuple-element.86), channel_id=1, source_target_pairs={{0,1},{1,0},{2,3},{3,2},{4,5},{5,4},{6,7},{7,6},{8,9},{9,8},{10,11... | collective-permute-start | bytes 221192 | tf_op jit(solution)/shard_map/ppermute | solution.py:264
  95.6 4.5 %collective-permute-start.10 = (f32[72,256]{1,0:T(8,128)S(1)}, f32[72,256]{1,0:T(8,128)S(1)}, u32[]{:S(2)}, u32[]{:S(2)}) collective-permute-start(f32[72,256]{1,0:T(8,128)S(1)} %add_add_fusion.1), channel_id=1, source_target_pairs={{0,8},{1,9},{2,10},{3,11},{4,12},{5,13},{6,14},{7,15},{8,0},{9,1},... | collective-permute-start | bytes 221192 | tf_op jit(solution)/shard_map/ppermute | solution.py:264
  96.0 9.7 %collective-permute-start.11 = (f32[72,256]{1,0:T(8,128)S(1)}, f32[72,256]{1,0:T(8,128)S(1)}, u32[]{:S(2)}, u32[]{:S(2)}) collective-permute-start(f32[72,256]{1,0:T(8,128)S(1)} %add_add_fusion.1), channel_id=1, source_target_pairs={{0,12},{1,13},{2,14},{3,15},{4,8},{5,9},{6,10},{7,11},{8,4},{9,5},... | collective-permute-start | bytes 221192 | tf_op jit(solution)/shard_map/ppermute | solution.py:264
  99.7 6.8 %collective-permute-start.9 = (f32[72,256]{1,0:T(8,128)S(1)}, f32[72,256]{1,0:T(8,128)S(1)}, u32[]{:S(2)}, u32[]{:S(2)}) collective-permute-start(f32[72,256]{1,0:T(8,128)S(1)} %add_add_fusion.1), channel_id=1, source_target_pairs={{0,4},{1,5},{2,6},{3,7},{4,0},{5,1},{6,2},{7,3},{8,12},{9,13},{10,... | collective-permute-start | bytes 221192 | tf_op jit(solution)/shard_map/ppermute | solution.py:264
  106.6 4.4 %collective-permute-start.12 = (f32[72,256]{1,0:T(8,128)S(1)}, f32[72,256]{1,0:T(8,128)S(1)}, u32[]{:S(2)}, u32[]{:S(2)}) collective-permute-start(f32[72,256]{1,0:T(8,128)S(1)} %add_add_fusion), channel_id=1, source_target_pairs={{0,16},{1,17},{2,18},{3,19},{4,20},{5,21},{6,22},{7,23},{8,24},{9,... | collective-permute-start | bytes 221192 | tf_op jit(solution)/shard_map/ppermute | solution.py:264
